TPU v7x, 32 devices: a whole 2x2x4 slice. The times are simulated.
32 devices in a mesh: dp: 4 (over z), fsdp: 8 (over y, x, core).
Axes of the slice: x: 2, y: 2, z: 4, core: 2. Of those that a mesh axis runs over, the one named last changes fastest.
Arguments:
- word_table: float32 [30720, 128], P(('dp', 'fsdp')), may hold values from -0.875 to 0.875
- position_table: float32 [512, 128], P(('dp', 'fsdp')), may hold values from -0.875 to 0.875
- head_weights: float32 [768, 1024], P(None, ('dp', 'fsdp'))
- decoder_bias: float32 [30720], P(('dp', 'fsdp')), may hold values from -1.25 to 1.25
- layer_wide: float32 [768, 6144], P(None, ('dp', 'fsdp'))
- layer_tall: float32 [3072, 768], P(('dp', 'fsdp')), may hold values from -0.109375 to 0.109375
- vectors: float32 [13184], replicated
- word_first: float32 [30720, 128], P(('dp', 'fsdp')), may hold values from -4.7683716e-07 to 4.7683716e-07
- word_second: float32 [30720, 128], P(('dp', 'fsdp')), may hold values from 5.2494893e-16 to 2.0997957e-15
- position_first: float32 [512, 128], P(('dp', 'fsdp')), may hold values from -4.7683716e-07 to 4.7683716e-07
- position_second: float32 [512, 128], P(('dp', 'fsdp')), may hold values from 5.2494893e-16 to 2.0997957e-15
- head_first: float32 [768, 1024], P(None, ('dp', 'fsdp')), may hold values from -9.536743e-07 to 9.536743e-07
- head_second: float32 [768, 1024], P(None, ('dp', 'fsdp')), may hold values from 2.0997957e-15 to 8.399183e-15
- decoder_first: float32 [30720], P(('dp', 'fsdp')), may hold values from -4.7683716e-07 to 4.7683716e-07
- decoder_second: float32 [30720], P(('dp', 'fsdp')), may hold values from 5.2494893e-16 to 2.0997957e-15
- wide_first: float32 [768, 6144], P(None, ('dp', 'fsdp')), may hold values from -9.536743e-07 to 9.536743e-07
- wide_second: float32 [768, 6144], P(None, ('dp', 'fsdp')), may hold values from 2.0997957e-15 to 8.399183e-15
- tall_first: float32 [3072, 768], P(('dp', 'fsdp')), may hold values from -9.536743e-07 to 9.536743e-07
- tall_second: float32 [3072, 768], P(('dp', 'fsdp')), may hold values from 2.0997957e-15 to 8.399183e-15
- vector_first: float32 [13184], replicated, may hold values from -3.8146973e-06 to 3.8146973e-06
- vector_second: float32 [13184], replicated, may hold values from 3.3596732e-14 to 1.3438693e-13
- token_ids: int32 [8192], P(('dp', 'fsdp')), may hold values from 0 to 30719
- seq_lengths: int32 [64], P(('dp', 'fsdp')), may hold values from 0 to 256, as said below
- mlm_rows: int32 [1280], P(('dp', 'fsdp')), may hold values from 0 to 255, as said below
- mlm_labels: int32 [1280], P(('dp', 'fsdp')), may hold values from -1 to 30719, as said below
- sop_labels: int32 [64], P(('dp', 'fsdp')), may hold values from 0 to 1
Outputs:
- word_new: float32 [30720, 128], P(('dp', 'fsdp'))
- word_first_new: float32 [30720, 128], P(('dp', 'fsdp'))
- word_second_new: float32 [30720, 128], P(('dp', 'fsdp'))
- position_new: float32 [512, 128], P(('dp', 'fsdp'))
- position_first_new: float32 [512, 128], P(('dp', 'fsdp'))
- position_second_new: float32 [512, 128], P(('dp', 'fsdp'))
- head_new: float32 [768, 1024], P(None, ('dp', 'fsdp'))
- head_first_new: float32 [768, 1024], P(None, ('dp', 'fsdp'))
- head_second_new: float32 [768, 1024], P(None, ('dp', 'fsdp'))
- decoder_new: float32 [30720], P(('dp', 'fsdp'))
- decoder_first_new: float32 [30720], P(('dp', 'fsdp'))
- decoder_second_new: float32 [30720], P(('dp', 'fsdp'))
- wide_new: float32 [768, 6144], P(None, ('dp', 'fsdp'))
- wide_first_new: float32 [768, 6144], P(None, ('dp', 'fsdp'))
- wide_second_new: float32 [768, 6144], P(None, ('dp', 'fsdp'))
- tall_new: float32 [3072, 768], P(('dp', 'fsdp'))
- tall_first_new: float32 [3072, 768], P(('dp', 'fsdp'))
- tall_second_new: float32 [3072, 768], P(('dp', 'fsdp'))
- vectors_new: float32 [13184], replicated
- vector_first_new: float32 [13184], replicated
- vector_second_new: float32 [13184], replicated
- mlm_sum: float32 [], replicated
- mlm_count: float32 [], replicated
- sop_sum: float32 [], replicated
- sop_count: float32 [], replicated
- grad_norm: float32 [], replicated
Inputs may be any that keep to these rules, and one draw needn't show every extreme that they name: `seq_lengths`: per device either one sequence of length l0 in (128, 256] with l1 = 0, or two sequences of lengths in [64, 128], the second starting at row 128. Some device holds a sequence of 256. `mlm_rows`: each slot names a live row of its own device's block. `mlm_labels`: -1 marks an unused slot; the others are word ids. Used slots come first on each device.
All inputs are finite; a program needn't handle non-finite values.
Results may differ from a plain program's by a relative error of at most 0.0085.
The roundings to bfloat16 on the way count: a program that leaves them out, or rounds other values in their place, can miss the bound.
Values may be sent and summed in bfloat16 or wider, within the bound.
A program may use at most 192 MiB of HBM per device.

v0:
```python
import functools

import jax
import jax.numpy as jnp
from jax import lax
from jax.experimental import pallas as pl
from jax.experimental.pallas import tpu as pltpu
from jax.sharding import PartitionSpec as P

D = 768
HEADS = 12
HEAD_DIM = 64
FF = 3072
E = 128
LAYERS = 4
STEP = 10
BUCKET = 128
ROWS = 2 * BUCKET

PRECISE = lax.Precision.HIGHEST
EPSILON = 1e-06
LEARN_RATE = 0.1
SMALL_RATE = 0.5
BETA_ONE = 0.9
BETA_TWO = 0.999
ADAM_EPSILON = 1e-08
WEIGHT_DECAY = 0.01
CLIP_NORM = 0.005
NORM_EPSILON = 1e-06
MASKED = -1e30
SCALE = HEAD_DIM ** (-0.5)
AXES = ("dp", "fsdp")


def to_half(x):
    return x.astype(jnp.bfloat16)


def product(a, b):
    return jnp.dot(a, b, preferred_element_type=jnp.float32)


def times_transpose(a, b):
    return lax.dot_general(a, b, (((1,), (1,)), ((), ())), preferred_element_type=jnp.float32)


def transpose_times(a, b):
    return lax.dot_general(a, b, (((0,), (0,)), ((), ())), preferred_element_type=jnp.float32)


def column_sum(x):
    return jnp.sum(x.astype(jnp.float32), 0)


def norm_forward(x):
    centre = x - jnp.mean(x, -1, keepdims=True)
    inverse = lax.rsqrt(jnp.mean(centre * centre, -1, keepdims=True) + EPSILON)
    return centre * inverse, inverse


def norm_backward(upstream, factor, hat, inverse):
    scaled = upstream * factor
    return inverse * (
        scaled
        - jnp.mean(scaled, -1, keepdims=True)
        - hat * jnp.mean(scaled * hat, -1, keepdims=True)
    )


GELU_A = 0.7978845608028654
GELU_B = 0.044715


MESH_ID = pl.DeviceIdType.MESH
VMEM_SPACE = pltpu.VMEM
VMEM_ASK = 60 * 1024 * 1024


def greet(peers):
    barrier = pltpu.get_barrier_semaphore()
    count = 0
    for present, who in peers:
        if present is None:
            pl.semaphore_signal(barrier, inc=1, device_id=who, device_id_type=MESH_ID)
            count = count + 1
        else:

            @pl.when(present)
            def _(who=who):
                pl.semaphore_signal(barrier, inc=1, device_id=who, device_id_type=MESH_ID)

            count = count + present.astype(jnp.int32)
    pl.semaphore_wait(barrier, count)


def maybe(condition, action):
    if condition is None:
        action()
    else:
        pl.when(condition)(action)


def remote(source, target, send, receive, who):
    return pltpu.make_async_remote_copy(
        src_ref=source,
        dst_ref=target,
        send_sem=send,
        recv_sem=receive,
        device_id=who,
        device_id_type=MESH_ID,
    )


OWN, ACROSS_X, ACROSS_Y, DIAGONAL = 0, 1, 2, 3


def cuts_of(rows):
    tail = max(32, round(rows * 0.22 / 32) * 32)
    head = rows - tail
    return ((0, head), (head, rows))


def half_of(span, which):
    low, high = span
    middle = (low + high) // 2
    return (low, middle) if which == 0 else (middle, high)


def places():
    z, f = lax.axis_index("dp"), lax.axis_index("fsdp")
    q, c = f // 2, lax.rem(f, 2)
    qx = q + 1 - 2 * lax.rem(q, 2)
    qy = lax.rem(q + 2, 4)
    qd = qx + qy - q
    return z, c, (q, qx, qy, qd)


def gather_stages(planes, rows, members, x, outs, buf, sems, where, opening):
    out_sem, send, recv, side_send, side_recv = sems
    z, c, cols = where
    cuts = cuts_of(rows)
    at_x, at_y, mate = (z, cols[1] * 2 + c), (z, cols[2] * 2 + c), (z, cols[0] * 2 + 1 - c)
    above, below = z < planes - 1, z > 0
    up, down = (z + 1, cols[0] * 2 + c), (z - 1, cols[0] * 2 + c)
    sent = []

    def block(zs, col, core, span):
        return buf.at[zs, cols[col], core, pl.ds(span[0], span[1] - span[0])]

    def push(condition, zs, col, span, who, slot, receive, mine=False):
        def make():
            here = block(zs, col, c, span)
            source = x.at[pl.ds(span[0], span[1] - span[0])] if mine else here
            return remote(source, here, send.at[slot[0], zs, slot[1]], receive, who)

        maybe(condition, lambda: make().start())
        sent.append((condition, make))

    def await_block(zs, col, span, receive, core=None):
        here = block(zs, col, c if core is None else core, span)
        remote(here, here, send.at[0, 0, 0], receive, mate).wait_recv()

    def deliver(zs, col, core, span):
        for index, (out, (low, high)) in enumerate(zip(outs, members)):
            first, last = max(low, span[0]), min(high, span[1])
            if first < last:
                pltpu.make_async_copy(
                    buf.at[zs, cols[col], core, pl.ds(first, last - first)],
                    out.at[zs, cols[col], core, pl.ds(first - low, last - first)],
                    out_sem.at[index],
                ).start()

    def share(condition, part, zs, col, span, kind, mine=False):
        def make():
            here = block(zs, col, c, span)
            source = x.at[pl.ds(span[0], span[1] - span[0])] if mine else here
            return remote(
                source, here, side_send.at[part, zs, kind], side_recv.at[part, zs, kind], mate
            )

        def action():
            make().start()
            if not mine:
                deliver(zs, col, c, span)

        maybe(condition, action)
        sent.append((condition, make))
        shared.append((condition, part, zs, col, span, kind))

    shared = []
    whole = [cuts[0], cuts[1]]
    for part in (0, 1):
        push(above, z, OWN, whole[part], up, (part, 2), recv.at[part, z, OWN], True)
        push(below, z, OWN, whole[part], down, (part, 3), recv.at[part, z, OWN], True)
    for part in (1, 0):
        if part == 0:
            opening()
        push(None, z, OWN, whole[part], at_x, (part, 0), recv.at[part, z, ACROSS_X], True)
        push(None, z, OWN, whole[part], at_y, (part, 1), recv.at[part, z, ACROSS_Y], True)
    for part in (0, 1):
        share(None, part, z, OWN, whole[part], 0, True)
    own_copy = pltpu.make_async_copy(x, buf.at[z, cols[0], c], out_sem.at[len(members)])
    own_copy.start()

    def turn(condition, part, zs):
        span = whole[part]
        for col, which, who, slot in ((ACROSS_X, 1, at_y, 4), (ACROSS_Y, 0, at_x, 5)):
            maybe(
                condition,
                lambda col=col: await_block(zs, col, span, recv.at[part, zs, col]),
            )
            push(condition, zs, col, half_of(span, which), who, (part, slot), recv.at[part, zs, 4 + which])
            if part == 1:
                push(above, zs, col, span, up, (1, 4 + 2 * col), recv.at[1, zs, col])
                push(below, zs, col, span, down, (1, 5 + 2 * col), recv.at[1, zs, col])
            share(condition, part, zs, col, span, col)

    yield
    turn(None, 1, z)
    yield
    for which in (0, 1):
        await_block(z, DIAGONAL, half_of(whole[1], which), recv.at[1, z, 4 + which])
    push(above, z, DIAGONAL, whole[1], up, (1, 10), recv.at[1, z, DIAGONAL])
    push(below, z, DIAGONAL, whole[1], down, (1, 11), recv.at[1, z, DIAGONAL])
    share(None, 1, z, DIAGONAL, whole[1], 3)
    yield
    turn(None, 0, z)

    def settle(upto):
        while len(shared) > upto:
            condition, part, zs, col, span, kind = shared.pop(0)

            def action():
                await_block(zs, col, span, side_recv.at[part, zs, kind], 1 - c)
                deliver(zs, col, 1 - c, span)

            maybe(condition, action)

    for step in range(1, planes):
        yield
        ways = ((z - step >= 0, z - step, above, up), (z + step < planes, z + step, below, down))
        for valid, zs, further, onward in ways:
            go = jnp.logical_and(valid, further)
            pl.when(valid)(
                lambda zs=zs: await_block(zs, OWN, whole[0], recv.at[0, zs, OWN])
            )
            push(go, zs, OWN, whole[0], onward, (0, 2), recv.at[0, zs, OWN])
            push(valid, zs, OWN, whole[0], at_x, (0, 0), recv.at[0, zs, ACROSS_X])
            push(valid, zs, OWN, whole[0], at_y, (0, 1), recv.at[0, zs, ACROSS_Y])
            share(valid, 0, zs, OWN, whole[0], 0)
        yield
        for valid, zs, further, onward in ways:
            go = jnp.logical_and(valid, further)
            for col in (OWN, ACROSS_X, ACROSS_Y, DIAGONAL):
                pl.when(valid)(
                    lambda zs=zs, col=col: await_block(zs, col, whole[1], recv.at[1, zs, col])
                )
                push(go, zs, col, whole[1], onward, (1, col), recv.at[1, zs, col])
                share(valid, 1, zs, col, whole[1], col)
        yield
        for valid, zs, further, onward in ways:
            turn(valid, 0, zs)
        settle(8)
    yield
    own_copy.wait()
    deliver(z, OWN, c, (0, rows))
    everywhere = [(None, z)] + [
        (valid, zs)
        for step in range(1, planes)
        for valid, zs in ((z - step >= 0, z - step), (z + step < planes, z + step))
    ]
    for condition, zs in everywhere:
        for which in (0, 1):
            span = half_of(whole[0], which)
            maybe(
                condition,
                lambda zs=zs, which=which, span=span: await_block(
                    zs, DIAGONAL, span, recv.at[0, zs, 4 + which]
                ),
            )
            share(condition, 0, zs, DIAGONAL, span, 3 + which)
    settle(0)
    for condition, make in sent:
        maybe(condition, lambda make=make: make().wait_send())
    for index, (out, (low, high)) in enumerate(zip(outs, members)):
        pltpu.make_async_copy(
            buf.at[:, :, :, pl.ds(low, high - low)], out, out_sem.at[index]
        ).wait()


def select_stages(planes, facts, own_word, found, refs, where, offset):
    part, side, plane_in, middle, line_in, turned, sems_send, sems_recv = refs
    z, c, cols = where
    q = cols[0]
    f = q * 2 + c
    mate = (z, q * 2 + 1 - c)
    words = own_word.shape[0]
    line = [(lax.rem(z + d, planes), f) for d in range(1, planes)]
    turned[...] = to_half(own_word[...].T)
    yield

    def mate_message(col):
        return remote(
            part.at[:, col, 1 - c], side.at[:, col], sems_send.at[0, col], sems_recv.at[0, col], mate
        )

    def plane_message(col):
        return remote(
            part.at[:, col, c],
            plane_in.at[col],
            sems_send.at[1, col],
            sems_recv.at[1, col],
            (z, cols[col] * 2 + c),
        )

    def line_message(d, who):
        return remote(
            middle.at[who[0]], line_in.at[d], sems_send.at[2, d], sems_recv.at[2, d], who
        )

    def merge(col):
        mate_message(col).wait_recv()
        for zt in range(planes):
            part[zt, col, c] = part[zt, col, c] + side[zt, col]
        if col != OWN:
            plane_message(col).start()

    order = (DIAGONAL, ACROSS_X, ACROSS_Y, OWN)
    for place, col in enumerate(order):

        def body(n, unused, col=col):
            zt, core = n // 2, lax.rem(n, 2)
            ids = facts[zt, cols[col] * 2 + core]
            row = lax.broadcasted_iota(jnp.int32, (words, BUCKET), 0) + offset
            picks = jnp.concatenate(
                [to_half((row == ids[i : i + 1, :]).astype(jnp.float32)) for i in (0, 1)], 1
            )
            part[zt, col, core] = to_half(nn(turned[...], picks))
            return unused

        lax.fori_loop(0, 2 * planes, body, 0)
        mate_message(col).start()
        if place > 0:
            merge(order[place - 1])
        yield
    merge(OWN)
    total = part[:, OWN, c]
    yield
    for col in order[:3]:
        plane_message(col).wait_recv()
        total = total + plane_in[col]
    middle[...] = total
    for d, who in enumerate(line):
        line_message(d, who).start()
    yield
    total = middle[z]
    for d, who in enumerate(line):
        line_message(d, who).wait_recv()
        total = total + line_in[d]
    found[...] = total.astype(jnp.float32).T
    for col in order:
        mate_message(col).wait_send()
    for col in order[:3]:
        plane_message(col).wait_send()
    for d, who in enumerate(line):
        line_message(d, who).wait_send()


PLAN = (1, 1, 1, 1, 1, 1, 1, 1, 1, 1, 1, 1, 1, 1)


def start_kernel(
    planes,
    rows,
    members,
    own_wide,
    own_tall,
    own_head,
    own_word,
    own_facts,
    own_place,
    *refs,
):
    width = 8
    count = len(members)
    outs, (facts, place, found) = refs[:count], refs[count : count + 3]
    x, buf = refs[count + 3 : count + 5]
    gather_sems = refs[count + 5 : count + 10]
    select_refs = refs[count + 10 : count + 18]
    line_send, line_recv, plane_send, plane_recv = refs[count + 18 :]
    where = places()
    z, c, cols = where
    f = cols[0] * 2 + c
    line = [(lax.rem(z + d, planes), f) for d in range(1, planes)]
    plane = [(z, lax.rem(f + d, width)) for d in range(1, width)]
    facts[z, f] = own_facts[...]
    place[z, f] = to_half(own_place[...]).astype(jnp.float32)
    greet([(None, who) for who in line + plane])
    pairs = (facts, place)

    def along(i, d, who):
        here = pairs[i].at[z, f]
        return remote(here, here, line_send.at[i, d], line_recv.at[i, d], who)

    def around(i, d, who, source):
        here = pairs[i].at[:, source]
        return remote(here, here, plane_send.at[i, d], plane_recv.at[i, d], who)

    for d, who in enumerate(line):
        for i in (0, 1):
            along(i, d, who).start()
    for (low, high), piece in zip(members, (own_wide[...], own_tall[...], own_head[...])):
        x[low:high] = to_half(piece)

    def opening():
        for d, who in enumerate(line):
            for i in (0, 1):
                source = pairs[i].at[lax.rem(z - d - 1 + planes, planes), f]
                remote(source, source, line_send.at[i, d], line_recv.at[i, d], who).wait_recv()
        for d, who in enumerate(plane):
            for i in (0, 1):
                around(i, d, who, f).start()

    gather = gather_stages(planes, rows, members, x, outs, buf, gather_sems, where, opening)
    offset = (z * width + f) * own_word.shape[0]
    select = select_stages(planes, facts, own_word, found, select_refs, where, offset)
    done = object()
    next(gather)
    next(select)
    for d in range(1, width):
        source = lax.rem(f - d + width, width)
        for i in (0, 1):
            around(i, d - 1, mate_of(where), source).wait_recv()
    for number in range(64):
        for unused in range(PLAN[number] if number < len(PLAN) else 1):
            next(select, done)
        if next(gather, done) is done:
            break
    for unused in select:
        pass
    for d, who in enumerate(line):
        for i in (0, 1):
            along(i, d, who).wait_send()
    for d, who in enumerate(plane):
        for i in (0, 1):
            around(i, d, who, f).wait_send()


def mate_of(where):
    z, c, cols = where
    return (z, cols[0] * 2 + 1 - c)


def run_start(shards, own_word, own_facts, own_place, mesh_shape, identity):
    planes, width = mesh_shape
    heights = tuple(shard.shape[0] for shard in shards)
    rows, columns = sum(heights), shards[1].shape[1]
    members, low = [], 0
    for height in heights:
        members.append((low, low + height))
        low += height
    half, single = jnp.bfloat16, jnp.float32
    vmem = pl.BlockSpec(memory_space=VMEM_SPACE)
    dma = pltpu.SemaphoreType.DMA
    words, features = own_word.shape
    block = (features, ROWS)
    *outs, facts, place, found = pl.pallas_call(
        functools.partial(start_kernel, planes, rows, tuple(members)),
        out_shape=[
            jax.ShapeDtypeStruct((planes, width // 2, 2, height, columns), half)
            for height in heights
        ]
        + [
            jax.ShapeDtypeStruct((planes, width, *own_facts.shape), own_facts.dtype),
            jax.ShapeDtypeStruct((planes, width, *own_place.shape), own_place.dtype),
            jax.ShapeDtypeStruct((ROWS, features), single),
        ],
        in_specs=[vmem] * 6,
        out_specs=[pl.BlockSpec(memory_space=pl.ANY)] * len(heights) + [vmem] * 3,
        scratch_shapes=[
            VMEM_SPACE((rows, columns), half),
            VMEM_SPACE((planes, width // 2, 2, rows, columns), half),
            dma((len(heights) + 1,)),
            dma((2, planes, 12)),
            dma((2, planes, 6)),
            dma((2, planes, 5)),
            dma((2, planes, 5)),
            VMEM_SPACE((planes, 4, 2, *block), half),
            VMEM_SPACE((planes, 4, *block), half),
            VMEM_SPACE((4, planes, *block), half),
            VMEM_SPACE((planes, *block), half),
            VMEM_SPACE((planes - 1, *block), half),
            VMEM_SPACE((features, words), half),
            dma((3, 4)),
            dma((3, 4)),
            dma((2, planes)),
            dma((2, planes)),
            dma((2, width)),
            dma((2, width)),
        ],
        compiler_params=pltpu.CompilerParams(
            collective_id=identity, has_side_effects=True, vmem_limit_bytes=VMEM_ASK
        ),
    )(*shards, own_word, own_facts, own_place)
    weights = [out.reshape(-1, columns) for out in outs]
    devices = planes * width
    return (
        weights,
        facts.reshape(devices, *own_facts.shape),
        place.reshape(devices, *own_place.shape),
        found,
    )


def accumulate(target, sources, height):
    step = 32

    def body(i, unused):
        rows = pl.ds(pl.multiple_of(i * step, step), step)
        total = sources[0][rows].astype(jnp.float32)
        for source in sources[1:]:
            total = total + source[rows].astype(jnp.float32)
        target[rows] = total.astype(target.dtype)
        return unused

    lax.fori_loop(0, height // step, body, 0)


ROWS_AT = 1
MATE_AT = 9


def far_first(i, z, planes):
    low = (2 * z < planes).astype(jnp.int32)
    falling = planes - 1 - i - (i >= planes - 1 - z).astype(jnp.int32)
    rising = i + (i >= z).astype(jnp.int32)
    last = (jnp.int32(i) == planes - 1).astype(jnp.int32)
    return last * z + (1 - last) * (low * falling + (1 - low) * rising)


def finish_kernel(
    planes,
    heights,
    split,
    left_wide,
    left_tall,
    rights,
    outer,
    head_grad,
    own_rows,
    vector_terms,
    facts,
    base_word,
    back_decoder,
    totals,
    out,
    word_grad,
    place_grad,
    last,
    ends,
    all_rows,
    both,
    side,
    half_in,
    full_in,
    line_in,
    tail_line,
    tail_half,
    tail_full,
    wide_buf,
    tall_buf,
    vector_in,
    vector_mid,
    vector_last,
    fetch,
    head_load,
    side_send,
    side_recv,
    send,
    recv,
    tail_send,
    tail_recv,
    row_send,
    row_recv,
    vec_send,
    vec_recv,
    end_send,
    end_recv,
):
    width = 8
    wide_height, tall_height, head_height = heights
    rows = wide_height + tall_height + head_height
    z, c, cols = places()
    q = cols[0]
    f = q * 2 + c
    x, y = lax.rem(q, 2), q // 2
    cuts = cuts_of(rows)
    head, tail = cuts
    head_rows, tail_rows = head[1] - head[0], tail[1] - tail[0]
    at_x, at_y, mate = (z, cols[1] * 2 + c), (z, cols[2] * 2 + c), (z, q * 2 + 1 - c)
    above, below = z < planes - 1, z > 0
    up, down = (z + 1, f), (z - 1, f)
    line = [(lax.rem(z + d, planes), f) for d in range(1, planes)]
    plane = [(z, lax.rem(f + d, width)) for d in range(1, width)]
    greet([(None, who) for who in line + plane])
    order = (DIAGONAL, ACROSS_X, ACROSS_Y, OWN)
    sent = []

    def push(condition, make):
        maybe(condition, lambda: make().start())
        sent.append((condition, make))

    def piece(ref, span):
        return ref.at[pl.ds(span[0], span[1] - span[0])]

    def plane_at(i):
        return far_first(i, z, planes)

    def turn_of(n):
        m = n - 1 - 3 * (n == 0).astype(jnp.int32) + (n > 4 * planes - 4).astype(jnp.int32)
        group, j = (m + 4) // 4 - 1, lax.rem(m + 4, 4)
        ahead = (j == 0).astype(jnp.int32)
        return group + ahead, DIAGONAL * ahead + j * (j < 3).astype(jnp.int32)

    def chip_of(n):
        i, col = turn_of(n)
        flip_x, flip_y = lax.rem(col, 2), col // 2
        return plane_at(i) * 4 + 2 * lax.rem(y + flip_y, 2) + lax.rem(x + flip_x, 2)

    def fetches(n):
        k, slot = chip_of(n), lax.rem(n, 2)
        wide_rows = pl.ds(pl.multiple_of(k * 2 * wide_height, 16), 2 * wide_height)
        tall_rows = pl.ds(pl.multiple_of(k * 2 * tall_height, 16), 2 * tall_height)
        return (
            pltpu.make_async_copy(
                left_wide.at[wide_rows], wide_buf.at[slot], fetch.at[0, slot]
            ),
            pltpu.make_async_copy(
                left_tall.at[tall_rows], tall_buf.at[slot], fetch.at[1, slot]
            ),
        )

    for copy in fetches(jnp.int32(0)):
        copy.start()

    def vector_first(d, who):
        return remote(
            vector_terms.at[:, who[1]], vector_in.at[d], vec_send.at[0, d], vec_recv.at[0, d], who
        )

    def vector_second(d, who):
        return remote(
            vector_mid.at[who[0]], vector_last.at[d], vec_send.at[1, d], vec_recv.at[1, d], who
        )

    def row_line(d, who):
        return remote(
            own_rows, all_rows.at[z, q, c], row_send.at[0, d], row_recv.at[0, d], who
        )

    def row_plane(col):
        return remote(
            all_rows.at[:, q, c],
            all_rows.at[:, q, c],
            row_send.at[1, col],
            row_recv.at[1, col],
            (z, cols[col] * 2 + c),
        )

    def row_mate():
        return remote(
            all_rows.at[:, :, c], all_rows.at[:, :, c], row_send.at[2, 0], row_recv.at[2, 0], mate
        )

    for d, who in enumerate(line):
        push(None, functools.partial(row_line, d, who))
    for d, who in enumerate(plane):
        push(None, functools.partial(vector_first, d, who))
    all_rows[z, q, c] = own_rows[...]
    head_copies = []
    for col in order:
        copy = pltpu.make_async_copy(
            head_grad.at[:, cols[col]],
            both.at[:, col, :, pl.ds(wide_height + tall_height, head_height)],
            head_load.at[col],
        )
        copy.start()
        head_copies.append(copy)

    def side_message(zt, col):
        return remote(
            both.at[zt, col, 1 - c],
            side.at[zt, col],
            side_send.at[col, zt],
            side_recv.at[col, zt],
            mate,
        )

    def half_message(zt, which):
        return remote(
            piece(both.at[zt, DIAGONAL, c], half_of(head, which)),
            half_in.at[which, zt],
            send.at[0, which, zt],
            recv.at[0, which, zt],
            (at_x, at_y)[which],
        )

    def full_message(zt, which):
        return remote(
            piece(both.at[zt, (ACROSS_X, ACROSS_Y)[which], c], head),
            full_in.at[which, zt],
            send.at[1, which, zt],
            recv.at[1, which, zt],
            (at_x, at_y)[which],
        )

    def line_message(zt, way):
        return remote(
            piece(both.at[zt, OWN, c], head),
            line_in.at[way, zt],
            send.at[2, way, zt],
            recv.at[2, way, zt],
            (up, down)[way],
        )

    def tail_message(zt, way):
        return remote(
            both.at[zt, :, c, pl.ds(tail[0], tail_rows)],
            tail_line.at[way, zt],
            tail_send.at[way, zt],
            tail_recv.at[way, zt],
            (up, down)[way],
        )

    def merged(zt, col):
        side_message(zt, col).wait_recv()
        mine = both.at[zt, col, c]
        accumulate(mine, [mine, side.at[zt, col]], rows)

    def second(zt):
        for which, col in ((0, ACROSS_X), (1, ACROSS_Y)):
            half_message(zt, 1 - which).wait_recv()
            target = piece(both.at[zt, col, c], half_of(head, 1 - which))
            accumulate(target, [target, half_in.at[1 - which, zt]], head_rows // 2)
            full_message(zt, which).start()

    def tail_add(zt, way):
        tail_message(zt, way).wait_recv()
        for col in range(4):
            target = piece(both.at[zt, col, c], tail)
            accumulate(target, [target, tail_line.at[way, zt, col]], tail_rows)

    def onward(zt, add, message):
        for way, valid in ((0, zt > z), (1, zt < z)):
            behind = (below, above)[way]
            pl.when(jnp.logical_and(valid, behind))(functools.partial(add, zt, way))
            pl.when(valid)(lambda way=way: message(zt, way).start())

    def tail_step(zt):
        onward(zt, tail_add, tail_message)

    def line_add(zt, way):
        line_message(zt, way).wait_recv()
        mine = piece(both.at[zt, OWN, c], head)
        accumulate(mine, [mine, line_in.at[way, zt]], head_rows)

    def third(zt):
        for which in (0, 1):
            full_message(zt, which).wait_recv()
        base = [piece(both.at[zt, OWN, c], head), full_in.at[0, zt], full_in.at[1, zt]]
        accumulate(base[0], base, head_rows)
        onward(zt, line_add, line_message)

    def after(n):
        i, col = turn_of(n)
        zt = plane_at(i)
        merged(zt, col)

        @pl.when(col == DIAGONAL)
        def _():
            half_message(zt, 0).start()
            half_message(zt, 1).start()

        @pl.when(col == OWN)
        def _():
            second(zt)
            pl.when(i < planes - 1)(lambda: tail_step(zt))
            pl.when(i > 0)(lambda: third(plane_at(i - 1)))

    for copy in head_copies:
        copy.wait()

    def await_plane_rows():
        for step in (ACROSS_X, ACROSS_Y, DIAGONAL):
            here = all_rows.at[:, cols[step], c]
            remote(here, here, row_send.at[1, step], row_recv.at[1, step], mate).wait_recv()

    def body(n, unused):
        for copy in fetches(n):
            copy.wait()

        @pl.when(n + 1 < 4 * planes)
        def _():
            for copy in fetches(n + 1):
                copy.start()

        (i, col), k, slot = turn_of(n), chip_of(n), lax.rem(n, 2)
        zt = plane_at(i)
        region = (k >= split[0]).astype(jnp.int32) + (k >= split[1]).astype(jnp.int32)
        product_wide = to_half(nn(wide_buf[slot], rights[region]))
        both[zt, col, 0, :wide_height] = product_wide[:wide_height]
        both[zt, col, 1, :wide_height] = product_wide[wide_height:]
        product_tall = to_half(nn(tall_buf[slot], outer[...]))
        here = slice(wide_height, wide_height + tall_height)
        both[zt, col, 0, here] = product_tall[:tall_height]
        both[zt, col, 1, here] = product_tall[tall_height:]
        side_message(zt, col).start()
        pl.when(n > 0)(lambda: after(n - 1))

        @pl.when(n == ROWS_AT)
        def _():
            for d, who in enumerate(line):
                row_line(d, who).wait_recv()
            for step in (ACROSS_X, ACROSS_Y, DIAGONAL):
                row_plane(step).start()
            total = vector_terms[:, f]
            for d, who in enumerate(plane):
                vector_first(d, who).wait_recv()
                total = total + vector_in[d]
            vector_mid[...] = total
            for d, who in enumerate(line):
                vector_second(d, who).start()

        @pl.when(n == MATE_AT)
        def _():
            await_plane_rows()
            row_mate().start()

        return unused

    lax.fori_loop(0, 4 * planes, body, 0)
    after(jnp.int32(4 * planes - 1))
    here = all_rows.at[:, :, 1 - c]
    remote(here, here, row_send.at[2, 0], row_recv.at[2, 0], mate).wait_recv()
    words = word_grad.shape[0]
    offset = (z * width + f) * words

    def look_back(first, after):
        def body(n, unused):
            zt, chip = n // 4, lax.rem(n, 4)
            row = lax.broadcasted_iota(jnp.int32, (words, BUCKET), 0) + offset
            total = word_grad[...]
            for core in (0, 1):
                ids = facts[zt, chip * 2 + core]
                picks = jnp.concatenate(
                    [to_half((row == ids[i : i + 1, :]).astype(jnp.float32)) for i in (0, 1)], 1
                )
                total = total + nn(picks, all_rows[zt, chip, core])
            word_grad[...] = total
            return unused

        lax.fori_loop(first, after, body, 0)

    word_grad[...] = base_word[...]
    look_back(0, 2 * planes)
    targets = [plane_at(i) for i in range(planes)]

    def tail_half_message(which):
        return remote(
            piece(both.at[z, DIAGONAL, c], half_of(tail, which)),
            tail_half.at[which],
            tail_send.at[2, which],
            tail_recv.at[2, which],
            (at_x, at_y)[which],
        )

    def tail_full_message(which):
        return remote(
            piece(both.at[z, (ACROSS_X, ACROSS_Y)[which], c], tail),
            tail_full.at[which],
            tail_send.at[3, which],
            tail_recv.at[3, which],
            (at_x, at_y)[which],
        )

    pl.when(below)(lambda: tail_add(z, 0))
    pl.when(above)(lambda: tail_add(z, 1))
    for which in (0, 1):
        push(None, functools.partial(tail_half_message, which))
    look_back(2 * planes, 4 * planes)
    for which, col in ((1, ACROSS_X), (0, ACROSS_Y)):
        tail_half_message(which).wait_recv()
        target = piece(both.at[z, col, c], half_of(tail, which))
        accumulate(target, [target, tail_half.at[which]], tail_rows // 2)
    for which in (0, 1):
        push(None, functools.partial(tail_full_message, which))
    for which in (0, 1):
        full_message(z, which).wait_recv()
    goal = piece(out, head)
    accumulate(
        goal, [piece(both.at[z, OWN, c], head), full_in.at[0, z], full_in.at[1, z]], head_rows
    )
    for present, way in ((below, 0), (above, 1)):

        def add(way=way):
            line_message(z, way).wait_recv()
            accumulate(goal, [goal, line_in.at[way, z]], head_rows)

        pl.when(present)(add)
    for which in (0, 1):
        tail_full_message(which).wait_recv()
    accumulate(
        piece(out, tail),
        [piece(both.at[z, OWN, c], tail), tail_full.at[0], tail_full.at[1]],
        tail_rows,
    )
    total = vector_mid[z]
    for d, who in enumerate(line):
        vector_second(d, who).wait_recv()
        total = total + vector_last[d]
    height = place_grad.shape[0]
    own = z * width + f
    low_half = (own * height < BUCKET).astype(jnp.float32)
    high_half = (own * height < 2 * BUCKET).astype(jnp.float32) - low_half
    slot = pl.multiple_of(lax.rem(own * height, BUCKET), height)
    lane = lax.broadcasted_iota(jnp.int32, (1, 128), 1)
    grad = jnp.zeros((height, 128), jnp.float32)
    for zt in range(planes):
        for chip in range(4):
            for core in (0, 1):
                note = facts[zt, chip * 2 + core, 4:5, :]
                two = jnp.sum(
                    jnp.where(lane == 1, (note > 0).astype(jnp.float32), 0.0), 1, keepdims=True
                )
                lower = all_rows[zt, chip, core, pl.ds(slot, height)].astype(jnp.float32)
                upper = all_rows[zt, chip, core, pl.ds(BUCKET + slot, height)].astype(jnp.float32)
                grad = grad + low_half * (lower + two * upper) + high_half * (1.0 - two) * upper
    place_grad[...] = grad
    squares = jnp.sum(grad * grad) + jnp.sum(back_decoder[...] * back_decoder[...])
    squares = squares + jnp.sum(word_grad[...] * word_grad[...])
    squares = squares + jnp.sum(out[...] * out[...])
    last[z, f, 0:8] = total
    last[z, f, 8:16] = jnp.concatenate(
        [totals[...], jnp.where(lane == 0, squares, 0.0), jnp.zeros((6, 128), jnp.float32)], 0
    )
    first_copies, second_copies = [], []
    for d, who in enumerate(line):
        here = last.at[z, f]
        first_copies.append(remote(here, here, end_send.at[0, d], end_recv.at[0, d], who))
        first_copies[-1].start()
    for d, who in enumerate(line):
        here = last.at[lax.rem(z - d - 1 + planes, planes), f]
        remote(here, here, end_send.at[0, d], end_recv.at[0, d], who).wait_recv()
    for d, who in enumerate(plane):
        here = last.at[:, f]
        second_copies.append(remote(here, here, end_send.at[1, d], end_recv.at[1, d], who))
        second_copies[-1].start()
    for d, who in enumerate(plane):
        here = last.at[:, lax.rem(f - d - 1 + width, width)]
        remote(here, here, end_send.at[1, d], end_recv.at[1, d], who).wait_recv()
    summed = last[...]
    tails = jnp.sum(jnp.sum(summed[:, :, 8:16], 0), 0)
    squares = jnp.sum(summed[:, :, 0:8] * summed[:, :, 0:8]) + jnp.sum(tails[1:2, :])
    norm = jnp.sqrt(jnp.broadcast_to(squares, (1, 128)))
    factor = jnp.minimum(1.0, CLIP_NORM / (norm + NORM_EPSILON))
    mlm = totals[0:1, :] - jnp.sum(jnp.where(lane == 1, tails[0:1, :], 0.0))
    sop = jnp.zeros((1, 128), jnp.float32) + jnp.sum(jnp.where(lane == 2, tails[0:1, :], 0.0))
    ends[...] = jnp.concatenate(
        [norm, factor, mlm, sop, jnp.zeros((4, 128), jnp.float32)], 0
    )
    for copy in first_copies + second_copies:
        copy.wait_send()
    row_mate().wait_send()
    for condition, make in sent:
        maybe(condition, lambda make=make: make().wait_send())
    for zt in targets:
        for col in order:
            side_message(zt, col).wait_send()
        for which in (0, 1):
            half_message(zt, which).wait_send()
            full_message(zt, which).wait_send()
        for way, valid in ((0, zt > z), (1, zt < z)):

            def done(zt=zt, way=way):
                tail_message(zt, way).wait_send()
                line_message(zt, way).wait_send()

            pl.when(valid)(done)
    for step in (ACROSS_X, ACROSS_Y, DIAGONAL):
        row_plane(step).wait_send()
    for d, who in enumerate(line):
        vector_second(d, who).wait_send()


def run_finish(
    left_wide,
    left_tall,
    rights,
    outer,
    head_grad,
    own_rows,
    vector_terms,
    facts,
    base_word,
    back_decoder,
    totals,
    places_count,
    mesh_shape,
    identity,
):
    planes, width = mesh_shape
    devices = planes * width
    columns = outer.shape[1]
    heights = (
        left_wide.shape[0] // devices,
        left_tall.shape[0] // devices,
        head_grad.shape[0] // devices,
    )
    rows = sum(heights)
    long = left_wide.shape[1]
    split = (3 * D // (2 * heights[0]), 4 * D // (2 * heights[0]))
    head, tail = (high - low for low, high in cuts_of(rows))
    half, single = jnp.bfloat16, jnp.float32
    block = vector_terms.shape[1:]
    vmem = pl.BlockSpec(memory_space=VMEM_SPACE)
    any_space = pl.BlockSpec(memory_space=pl.ANY)
    dma = pltpu.SemaphoreType.DMA
    out, word_grad, place_grad, last, ends = pl.pallas_call(
        functools.partial(finish_kernel, planes, heights, split),
        out_shape=[
            jax.ShapeDtypeStruct((rows, columns), single),
            jax.ShapeDtypeStruct(base_word.shape, single),
            jax.ShapeDtypeStruct((places_count, 128), single),
            jax.ShapeDtypeStruct((planes, width, 16, 128), single),
            jax.ShapeDtypeStruct((8, 128), single),
        ],
        in_specs=[any_space, any_space, vmem, vmem, any_space, vmem, vmem] + [vmem] * 4,
        out_specs=[vmem] * 5,
        scratch_shapes=[
            VMEM_SPACE((planes, width // 2, 2, *own_rows.shape), half),
            VMEM_SPACE((planes, 4, 2, rows, columns), half),
            VMEM_SPACE((planes, 4, rows, columns), half),
            VMEM_SPACE((2, planes, head // 2, columns), half),
            VMEM_SPACE((2, planes, head, columns), half),
            VMEM_SPACE((2, planes, head, columns), half),
            VMEM_SPACE((2, planes, 4, tail, columns), half),
            VMEM_SPACE((2, tail // 2, columns), half),
            VMEM_SPACE((2, tail, columns), half),
            VMEM_SPACE((2, 2 * heights[0], long), half),
            VMEM_SPACE((2, 2 * heights[1], long), half),
            VMEM_SPACE((width - 1, planes, *block), single),
            VMEM_SPACE((planes, *block), single),
            VMEM_SPACE((planes - 1, *block), single),
            dma((2, 2)),
            dma((4,)),
            dma((4, planes)),
            dma((4, planes)),
            dma((3, 2, planes)),
            dma((3, 2, planes)),
            dma((4, planes)),
            dma((4, planes)),
            dma((3, 4)),
            dma((3, 4)),
            dma((2, width)),
            dma((2, width)),
            dma((2, width)),
            dma((2, width)),
        ],
        compiler_params=pltpu.CompilerParams(
            collective_id=identity, has_side_effects=True, vmem_limit_bytes=VMEM_ASK
        ),
    )(
        left_wide,
        left_tall,
        rights,
        outer,
        head_grad.reshape(planes, width // 2, 2, heights[2], columns),
        own_rows,
        vector_terms.reshape(planes, width, *block),
        facts.reshape(planes, width, *facts.shape[1:]),
        base_word,
        back_decoder,
        totals,
    )
    return out, heights, word_grad, place_grad, last, ends


LIFT = 128
WIRE = 48


def exact_rows(pick, values):
    first = to_half(values)
    rest = values - first.astype(jnp.float32)
    second = to_half(rest)
    third = to_half(rest - second.astype(jnp.float32))
    return nn(pick, first) + nn(pick, second) + nn(pick, third)


def lanes_to_rows(x):
    return jnp.concatenate([x[:, i : i + 128] for i in range(0, x.shape[1], 128)], 0)


def rows_to_lanes(x):
    return jnp.concatenate([x[i : i + 1] for i in range(x.shape[0])], 1)


def head_kernel(
    planes,
    lengths,
    sop_labels,
    final,
    head,
    word,
    decoder,
    facts,
    own_facts,
    vec,
    back_final,
    back_word,
    back_decoder,
    back_head,
    wide_sums,
    small_sums,
    totals,
    all_t,
    stats,
    powers,
    back_t,
    plane_in,
    middle,
    line_in,
    word_half,
    sends,
    recvs,
):
    width = 8
    z, c, cols = places()
    f = cols[0] * 2 + c
    line = [(lax.rem(z + d, planes), f) for d in range(1, planes)]
    plane = [(z, lax.rem(f + d, width)) for d in range(1, width)]
    greet([(None, who) for who in line + plane])
    offset = (z * width + f) * word.shape[0]
    words, slots = word.shape[0], planes * width * WIRE
    single = jnp.float32

    def gather_line(ref, kind):
        here = ref.at[z, f]
        return [
            remote(here, here, sends.at[kind, d], recvs.at[kind, d], who)
            for d, who in enumerate(line)
        ]

    def gather_plane(ref, kind):
        here = ref.at[:, f]
        return [
            remote(here, here, sends.at[kind, d], recvs.at[kind, d], who)
            for d, who in enumerate(plane)
        ]

    def await_line(ref, kind):
        for d in range(planes - 1):
            here = ref.at[lax.rem(z - d - 1 + planes, planes), f]
            remote(here, here, sends.at[kind, d], recvs.at[kind, d], line[d]).wait_recv()

    def await_plane(ref, kind):
        for d in range(width - 1):
            here = ref.at[:, lax.rem(f - d - 1 + width, width)]
            remote(here, here, sends.at[kind, d], recvs.at[kind, d], plane[d]).wait_recv()

    started = []
    lane = lax.broadcasted_iota(jnp.int32, (1, 128), 1)
    notes = facts[...]
    labels = jnp.concatenate([notes[i, 2:3, :WIRE] for i in range(planes * width)], 1)
    used = (lanes_to_rows(labels) >= 0).astype(single)
    mlm_count = jnp.sum(used)
    seconds = jnp.where(lane == 1, (notes[:, 4, :] > 0).astype(single), 0.0)
    sop_count = planes * width + jnp.sum(seconds)
    mlm_scale = 1.0 / jnp.broadcast_to(mlm_count, (1, 1))
    sop_scale = 1.0 / jnp.broadcast_to(sop_count, (1, 1))

    def start(copies):
        for copy in copies:
            copy.start()
        started.extend(copies)

    final_half = to_half(final[...])
    place = lax.broadcasted_iota(jnp.int32, (ROWS, LIFT), 0)
    scatter = to_half((place == own_facts[3:4, :]).astype(single))
    pick = scatter.T
    picked = to_half(nn(pick, final_half))
    dense = nt(picked, head[:E, :]) + short_row(vec, MLM_B)
    bend = jnp.tanh(GELU_A * dense * (1.0 + GELU_B * dense * dense))
    hat, inverse = norm_forward(0.5 * dense * (1.0 + bend))
    slope = 0.5 * (1.0 + bend) + (0.5 * GELU_A) * dense * (1.0 - bend * bend) * (
        1.0 + 3.0 * GELU_B * dense * dense
    )
    rows_half = to_half(hat * short_row(vec, MLM_G) + short_row(vec, MLM_LB))
    all_t[z, f] = rows_half[:WIRE]
    start(gather_line(all_t, 0))

    word_half[...] = to_half(word[...])
    row16 = lax.broadcasted_iota(jnp.int32, (16, ROWS), 0)
    col16 = lax.broadcasted_iota(jnp.int32, (16, ROWS), 1)
    leads = to_half(
        (jnp.logical_and(row16 < 2, col16 == row16 * BUCKET)).astype(single)
    )
    firsts = to_half(nn(leads, final_half))
    pooled = jnp.tanh(nt(firsts, head[E : E + D, :]) + wide_row(vec, POOL_B))
    await_line(all_t, 0)
    start(gather_plane(all_t, 1))
    zero_class, one_class = lanes_of(vec, CLS_AT, D // 128), lanes_of(vec, CLS_AT + D // 128, D // 128)
    c0 = jnp.sum(pooled * zero_class, -1, keepdims=True)
    c1 = jnp.sum(pooled * one_class, -1, keepdims=True)
    class_top = jnp.maximum(c0, c1)
    e0, e1 = jnp.exp(c0 - class_top), jnp.exp(c1 - class_top)
    class_total = e0 + e1
    which = lax.broadcasted_iota(jnp.int32, (16, 1), 0)
    label = jnp.where(which == 0, sop_labels[0], sop_labels[1])
    hit = (label == 1).astype(single)
    two = (lengths[1] > 0).astype(single)
    present = jnp.where(which == 0, 1.0, jnp.where(which == 1, two, 0.0))
    losses = (jnp.log(class_total) + class_top - (c0 + hit * (c1 - c0))) * present
    weight = present * sop_scale
    back_c0 = (e0 / class_total - (1.0 - hit)) * weight
    back_c1 = (e1 / class_total - hit) * weight
    wide_sums[1:2, :] = jnp.sum(back_c0 * pooled, 0, keepdims=True)
    wide_sums[2:3, :] = jnp.sum(back_c1 * pooled, 0, keepdims=True)
    pre_half = to_half((back_c0 * zero_class + back_c1 * one_class) * (1.0 - pooled * pooled))
    wide_sums[0:1, :] = jnp.sum(pre_half.astype(single), 0, keepdims=True)
    back_head[E : E + D, :] = to_half(tn(pre_half, firsts))
    back_firsts = nn(pre_half, head[E : E + D, :])
    await_plane(all_t, 1)

    row = lax.broadcasted_iota(jnp.int32, (words, 128), 0) + offset
    bias = jnp.broadcast_to(to_half(decoder[...]).astype(single), (8, words)).T[:, 0:1]
    tops, sums, targets = [], [], []
    chunk = width * WIRE
    flat_t = all_t[...].reshape(slots, E)
    for low in range(0, slots, chunk):
        logits = nt(word_half[...], flat_t[low : low + chunk]) + bias
        top = jnp.max(logits, 0, keepdims=True)
        power = jnp.exp(logits - top)
        powers[:, pl.ds(low, chunk)] = power
        tops.append(top)
        sums.append(jnp.sum(power, 0, keepdims=True))
        for at in range(0, chunk, 128):
            mark = row == labels[:, low + at : low + at + 128]
            targets.append(
                jnp.sum(jnp.where(mark, logits[:, at : at + 128], 0.0), 0, keepdims=True)
            )
    own_top = lanes_to_rows(jnp.concatenate(tops, 1))
    groups = slots // 128
    stats[z, f, 0:groups] = own_top
    stats[z, f, groups : 2 * groups] = lanes_to_rows(jnp.concatenate(sums, 1))
    start(gather_line(stats, 2))
    target = jnp.sum(jnp.concatenate(targets, 0) * used)
    await_line(stats, 2)
    start(gather_plane(stats, 3))
    await_plane(stats, 3)
    every = stats[...].reshape(planes * width, 2 * groups, 128)
    top = jnp.max(every[:, :groups], 0)
    total = jnp.sum(every[:, groups:] * jnp.exp(every[:, :groups] - top[None]), 0)
    log_sum = jnp.sum((jnp.log(total) + top) * used)
    weight = used * mlm_scale
    factor = rows_to_lanes(weight * jnp.exp(own_top - top) / total)
    weight = rows_to_lanes(weight)

    def slot_terms(zz, d, who):
        return remote(
            back_t.at[zz, who[1]],
            plane_in.at[d, zz],
            sends.at[4 + zz, d],
            recvs.at[4 + zz, d],
            who,
        )

    words_total = jnp.zeros((words, E), single)
    word_sums = jnp.zeros((8, words), single)
    ones = jnp.ones((8, width * WIRE), jnp.bfloat16)
    for low in range(0, slots, chunk):
        parts = []
        for at in range(low, low + chunk, 128):
            mark = row == labels[:, at : at + 128]
            part = powers[:, pl.ds(at, 128)] * factor[:, at : at + 128] - jnp.where(
                mark, weight[:, at : at + 128], 0.0
            )
            parts.append(to_half(part))
        half = jnp.concatenate(parts, 1)
        word_sums = word_sums + nt(ones, half)
        words_total = words_total + nn(half, flat_t[low : low + chunk])
        zz = low // chunk
        back_t[zz] = tn(half, word_half[...]).reshape(width, WIRE, E)
        start([slot_terms(zz, d, who) for d, who in enumerate(plane)])
    back_word[...] = words_total
    back_decoder[...] = word_sums[0:1]

    for zz in range(planes):
        total = back_t[zz, f]
        for d in range(width - 1):
            slot_terms(zz, d, plane[d]).wait_recv()
            total = total + plane_in[d, zz]
        middle[zz] = total
    start(
        [
            remote(middle.at[who[0]], line_in.at[d], sends.at[4 + planes, d], recvs.at[4 + planes, d], who)
            for d, who in enumerate(line)
        ]
    )
    total = middle[z]
    for d in range(planes - 1):
        remote(
            line_in.at[d], line_in.at[d], sends.at[4 + planes, d], recvs.at[4 + planes, d], line[d]
        ).wait_recv()
        total = total + line_in[d]
    back_rows = jnp.concatenate([total, jnp.zeros((LIFT - WIRE, E), single)], 0)
    small_sums[1:2, :] = jnp.sum(back_rows * hat, 0, keepdims=True)
    small_sums[2:3, :] = jnp.sum(back_rows, 0, keepdims=True)
    dense_half = to_half(norm_backward(back_rows, short_row(vec, MLM_G), hat, inverse) * slope)
    small_sums[0:1, :] = jnp.sum(dense_half.astype(single), 0, keepdims=True)
    back_head[:E, :] = to_half(tn(dense_half, picked))
    back_final[...] = exact_rows(scatter, nn(dense_half, head[:E, :]))
    back_final[0:1, :] = back_final[0:1, :] + back_firsts[0:1]
    back_final[BUCKET : BUCKET + 1, :] = back_final[BUCKET : BUCKET + 1, :] + back_firsts[1:2]
    sop_sum = jnp.sum(losses)
    ends = jnp.zeros((1, 128), single)
    for at, value in enumerate((log_sum, target, sop_sum, mlm_count, sop_count)):
        ends = ends + jnp.where(lane == at, value, 0.0)
    totals[...] = ends
    for copy in started:
        copy.wait_send()


def run_head(
    lengths, sop_labels, final, head, word, decoder, facts, own_facts, vec, mesh_shape, identity
):
    planes, width = mesh_shape
    words = word.shape[0]
    slots = planes * width * WIRE
    groups = slots // 128
    single, half = jnp.float32, jnp.bfloat16
    vmem = pl.BlockSpec(memory_space=VMEM_SPACE)
    smem = pl.BlockSpec(memory_space=pltpu.SMEM)
    dma = pltpu.SemaphoreType.DMA
    return pl.pallas_call(
        functools.partial(head_kernel, planes),
        out_shape=[
            jax.ShapeDtypeStruct((ROWS, D), single),
            jax.ShapeDtypeStruct((words, E), single),
            jax.ShapeDtypeStruct((1, words), single),
            jax.ShapeDtypeStruct(head.shape, half),
            jax.ShapeDtypeStruct((3, D), single),
            jax.ShapeDtypeStruct((3, E), single),
            jax.ShapeDtypeStruct((1, 128), single),
        ],
        in_specs=[smem] * 2 + [vmem] * 7,
        out_specs=[vmem] * 7,
        scratch_shapes=[
            VMEM_SPACE((planes, width, WIRE, E), half),
            VMEM_SPACE((planes, width, 2 * groups, 128), single),
            VMEM_SPACE((words, slots), single),
            VMEM_SPACE((planes, width, WIRE, E), single),
            VMEM_SPACE((width - 1, planes, WIRE, E), single),
            VMEM_SPACE((planes, WIRE, E), single),
            VMEM_SPACE((planes - 1, WIRE, E), single),
            VMEM_SPACE((words, E), half),
            dma((5 + planes, width)),
            dma((5 + planes, width)),
        ],
        compiler_params=pltpu.CompilerParams(
            collective_id=identity, has_side_effects=True, vmem_limit_bytes=VMEM_ASK
        ),
    )(lengths, sop_labels, final, head, word, decoder, facts, own_facts, vec)


def adam_update(weight, gradient, first, second, rate):
    first = BETA_ONE * first + (1 - BETA_ONE) * gradient
    second = BETA_TWO * second + (1 - BETA_TWO) * gradient * gradient
    first_hat = first / (1 - BETA_ONE**STEP)
    second_hat = second / (1 - BETA_TWO**STEP)
    updated = weight - rate * (
        first_hat / (jnp.sqrt(second_hat) + ADAM_EPSILON) + WEIGHT_DECAY * weight
    )
    return (updated, first, second)


def adam_kernel(blocks, rates, *refs):
    count = len(rates)
    ends, refs = refs[0], refs[1:]
    ins, outs = refs[: 4 * count], refs[4 * count :]
    factor = ends[1:2, 0:1]

    def update(number):
        weight, first, second, gradient = ins[4 * number : 4 * number + 4]
        grad = gradient[...]
        if grad.ndim > 2:
            grad = grad[:, :, :8].reshape(-1, 128)[: weight.shape[0]]
        results = adam_update(
            weight[...], factor * grad, first[...], second[...], rates[number]
        )
        for out, result in zip(outs[3 * number : 3 * number + 3], results):
            out[...] = result

    for number in range(blocks):
        update(number)

    @pl.when(pl.program_id(0) == 0)
    def _():
        for number in range(blocks, count):
            update(number)


def run_adam(ends, groups, steps):
    in_specs = [pl.BlockSpec(ends.shape, lambda i: (0, 0))]
    out_specs, shapes, given = [], [], [ends]
    blocks = 0
    for weight, first, second, gradient, low, rate in groups:
        rows, columns = weight.shape
        if low is None:
            spec = pl.BlockSpec(weight.shape, lambda i: (0, 0))
            zero = (0,) * gradient.ndim
            grad_spec = pl.BlockSpec(gradient.shape, lambda i, zero=zero: zero)
        else:
            blocks += 1
            height = rows // steps
            spec = pl.BlockSpec((height, columns), lambda i: (i, 0))
            grad_spec = pl.BlockSpec(
                (height, columns), lambda i, start=low // height: (start + i, 0)
            )
        in_specs += [spec] * 3 + [grad_spec]
        out_specs += [spec] * 3
        shapes += [jax.ShapeDtypeStruct(weight.shape, jnp.float32)] * 3
        given += [weight, first, second, gradient]
    return pl.pallas_call(
        functools.partial(adam_kernel, blocks, tuple(group[5] for group in groups)),
        grid=(steps,),
        out_shape=shapes,
        in_specs=in_specs,
        out_specs=out_specs,
        compiler_params=pltpu.CompilerParams(
            dimension_semantics=("arbitrary",), vmem_limit_bytes=VMEM_ASK
        ),
    )(*given)


class Network:
    def __init__(self, mesh):
        self.shape = (mesh.shape["dp"], mesh.shape["fsdp"])
        self.devices = self.shape[0] * self.shape[1]
        self.kernels = self.shape[1] == 8
        self.calls = 0

    def identity(self):
        self.calls += 1
        return self.calls

    def start(self, shards, own_word, own_facts, own_place):
        if self.kernels:
            return run_start(
                shards, own_word, own_facts, own_place, self.shape, self.identity()
            )
        weights = [lax.all_gather(to_half(w), AXES, axis=0, tiled=True) for w in shards]
        facts = lax.all_gather(own_facts, AXES)
        place = lax.all_gather(to_half(own_place), AXES).astype(jnp.float32)
        words = own_word.shape[0]
        ids = facts[:, : ROWS // 128].reshape(-1) - lax.axis_index(AXES) * words
        column = jnp.arange(words, dtype=jnp.int32)
        select = to_half(ids[:, None] == column[None, :])
        terms = product(select, to_half(own_word))
        found = lax.psum_scatter(terms, AXES, scatter_dimension=0, tiled=True)
        return weights, facts, place, found

    def head(self, lengths, sop_labels, final, head, word, decoder, facts, own_facts, vec):
        decoder = decoder[None]
        given = (lengths, sop_labels, final, head, word, decoder, facts, own_facts, vec)
        if self.kernels:
            return run_head(*given, self.shape, self.identity())
        return self.plain_head(*given)

    def plain_head(self, lengths, sop_labels, final, head, word, decoder, facts, own_facts, vec):
        short, cls = vec[SHORT_AT:], vec[CLS_AT:FF_AT].reshape(2, D)
        pool_b = vec[POOL_B * D // 128 : CLS_AT].reshape(D)
        labels = facts[:, 2, :WIRE].reshape(1, -1)
        mlm_count = jnp.sum((labels >= 0).astype(jnp.float32))
        sop_count = self.devices + jnp.sum((facts[:, 4, 1] > 0).astype(jnp.float32))
        single = jnp.float32
        offset = lax.axis_index(AXES) * word.shape[0]
        word_half, final_half = to_half(word), to_half(final)
        rows = own_facts[3, :WIRE]
        pick = (rows[:, None] == jnp.arange(ROWS, dtype=jnp.int32)[None]).astype(single)
        picked = to_half(product(to_half(pick), final_half))
        dense = times_transpose(picked, head[:E]) + short[MLM_B]
        bend = jnp.tanh(GELU_A * dense * (1.0 + GELU_B * dense * dense))
        hat, inverse = norm_forward(0.5 * dense * (1.0 + bend))
        slope = 0.5 * (1.0 + bend) + (0.5 * GELU_A) * dense * (1.0 - bend * bend) * (
            1.0 + 3.0 * GELU_B * dense * dense
        )
        rows_half = to_half(hat * short[MLM_G] + short[MLM_LB])
        all_rows = lax.all_gather(rows_half, AXES, axis=0, tiled=True)
        logits = times_transpose(word_half, all_rows) + to_half(decoder).astype(single).T
        mark = jnp.arange(word.shape[0], dtype=jnp.int32)[:, None] + offset == labels
        own_top = jnp.max(logits, 0)
        own_total = jnp.sum(jnp.exp(logits - own_top), 0)
        used = (labels[0] >= 0).astype(single)
        target = jnp.sum(jnp.sum(jnp.where(mark, logits, 0.0), 0) * used)
        top = lax.pmax(own_top, AXES)
        total = lax.psum(own_total * jnp.exp(own_top - top), AXES)
        log_sum = jnp.sum((jnp.log(total) + top) * used)
        weight = used / mlm_count
        half = to_half((jnp.exp(logits - top) / total - mark.astype(single)) * weight)
        back_rows = lax.psum_scatter(
            transpose_times(half, word_half), AXES, scatter_dimension=0, tiled=True
        )
        dense_half = to_half(norm_backward(back_rows, short[MLM_G], hat, inverse) * slope)
        back_final = lax.dot_general(
            pick, product(dense_half, head[:E]), (((0,), (0,)), ((), ())), precision=PRECISE
        )
        firsts = jnp.stack([final_half[0], final_half[BUCKET]])
        pooled = jnp.tanh(times_transpose(firsts, head[E : E + D]) + pool_b)
        classes = jnp.sum(pooled[:, None] * cls[None], -1)
        powers = jnp.exp(classes - jnp.max(classes, -1, keepdims=True))
        totals = jnp.sum(powers, -1, keepdims=True)
        onehot = jnp.stack([1 - sop_labels, sop_labels], 1).astype(single)
        present = jnp.stack([jnp.float32(1.0), (lengths[1] > 0).astype(single)])
        losses = jnp.log(totals[:, 0]) + jnp.max(classes, -1) - jnp.sum(classes * onehot, -1)
        back_classes = (powers / totals - onehot) * (present / sop_count)[:, None]
        back_pooled = jnp.sum(back_classes[:, :, None] * cls[None], 1)
        pre_half = to_half(back_pooled * (1.0 - pooled * pooled))
        back_firsts = product(pre_half, head[E : E + D])
        back_final = back_final.at[0].add(back_firsts[0]).at[BUCKET].add(back_firsts[1])
        back_cls = jnp.sum(back_classes[:, :, None] * pooled[:, None], 0)
        small_sums = [column_sum(dense_half), jnp.sum(back_rows * hat, 0), jnp.sum(back_rows, 0)]
        back_head = [transpose_times(dense_half, picked), transpose_times(pre_half, firsts)]
        ends = jnp.stack([log_sum, target, jnp.sum(losses * present), mlm_count, sop_count])
        return (
            back_final,
            product(half, all_rows),
            column_sum(half.T)[None],
            to_half(jnp.pad(jnp.concatenate(back_head, 0), ((0, E), (0, 0)))),
            jnp.concatenate([column_sum(pre_half)[None], back_cls], 0),
            jnp.stack(small_sums),
            jnp.pad(ends, (0, 123))[None],
        )

    def adam(self, ends, groups):
        if self.kernels:
            updates = run_adam(ends, groups, 4)
            return [updates[i : i + 3] for i in range(0, len(updates), 3)]
        updates = []
        for weight, first, second, gradient, low, rate in groups:
            rows = weight.shape[0]
            if low is not None:
                gradient = gradient[low : low + rows]
            gradient = gradient.reshape(-1, weight.shape[1])[:rows]
            updates.append(adam_update(weight, ends[1, 0] * gradient, first, second, rate))
        return updates

    def finish(
        self,
        left_wide,
        left_tall,
        rights,
        outer,
        head_grad,
        own_rows,
        vector,
        facts,
        base_word,
        back_decoder,
        totals,
        places_count,
    ):
        devices = self.devices
        if self.kernels:
            out, heights, word_grad, place_grad, last, ends = run_finish(
                left_wide,
                left_tall,
                rights,
                outer,
                head_grad,
                own_rows,
                vector,
                facts,
                base_word,
                back_decoder,
                totals,
                places_count,
                self.shape,
                self.identity(),
            )
            return out, heights, word_grad, place_grad, last, ends
        back_wide = jnp.concatenate(
            [
                product(left_wide[: 3 * D], rights[0]),
                product(left_wide[3 * D : 4 * D], rights[1]),
                product(left_wide[4 * D :], rights[2]),
            ],
            0,
        )
        sums = [
            lax.psum_scatter(p.astype(jnp.float32), AXES, scatter_dimension=0, tiled=True)
            for p in (back_wide, product(left_tall, outer), head_grad)
        ]
        all_rows = lax.all_gather(own_rows, AXES, axis=0, tiled=True)
        own, words = lax.axis_index(AXES), base_word.shape[0]
        ids = facts[:, : ROWS // 128].reshape(-1) - own * words
        select = to_half(ids[:, None] == jnp.arange(words, dtype=jnp.int32)[None, :])
        word_grad = base_word + transpose_times(select, all_rows)
        by_device = all_rows.reshape(devices, ROWS, E).astype(jnp.float32)
        two = (facts[:, 4, 1] > 0)[:, None, None]
        lower, upper = by_device[:, :BUCKET], by_device[:, BUCKET:]
        lower = jnp.sum(lower + jnp.where(two, upper, 0.0), 0)
        upper = jnp.sum(jnp.where(two, 0.0, upper), 0)
        every = jnp.concatenate([lower, upper], 0)
        every = jnp.pad(every, ((0, places_count * devices - ROWS), (0, 0)))
        place_grad = lax.dynamic_slice(every, (own * places_count, 0), (places_count, E))
        squares = sum(jnp.sum(g * g) for g in (*sums, word_grad, place_grad, back_decoder))
        reduced, tails, squares = lax.psum((vector, totals, squares), AXES)
        norm = jnp.sqrt(squares + jnp.sum(reduced * reduced))
        factor = jnp.minimum(1.0, CLIP_NORM / (norm + NORM_EPSILON))
        ends = jnp.stack([norm, factor, totals[0, 0] - tails[0, 1], tails[0, 2]])
        ends = jnp.broadcast_to(ends[:, None], (4, 128))
        heights = tuple(total.shape[0] for total in sums)
        return jnp.concatenate(sums, 0), heights, word_grad, place_grad, reduced, ends


CLS_AT, FF_AT, SHORT_AT = 10 * D // 128, 12 * D // 128, (12 * D + FF) // 128


def lanes_of(vec, first, count):
    return jnp.concatenate([vec[pl.ds(first + i, 1), :] for i in range(count)], 1)


def wide_row(vec, index):
    return lanes_of(vec, index * (D // 128), D // 128)


def short_row(vec, index):
    return vec[pl.ds(SHORT_AT + index, 1), :]


def nt(a, b):
    return lax.dot_general(a, b, (((1,), (1,)), ((), ())), preferred_element_type=jnp.float32)


def nn(a, b):
    return jnp.dot(a, b, preferred_element_type=jnp.float32)


def tn(a, b):
    return lax.dot_general(a, b, (((0,), (0,)), ((), ())), preferred_element_type=jnp.float32)


CHUNK = 512
PAIR = 2 * HEAD_DIM
PROJ_B, Q_B, V_B, O_B, LN1_G, LN1_B, FFO_B, LN2_G, LN2_B, POOL_B = range(10)


def allowed_block(lengths):
    shape = (ROWS, ROWS)
    row = lax.broadcasted_iota(jnp.int32, shape, 0)
    col = lax.broadcasted_iota(jnp.int32, shape, 1)
    two = lengths[1] > 0
    row_second = jnp.logical_and(row >= BUCKET, two).astype(jnp.int32)
    col_second = jnp.logical_and(col >= BUCKET, two).astype(jnp.int32)
    length = jnp.where(col_second == 1, lengths[1], lengths[0])
    live = col - BUCKET * col_second < length
    return jnp.logical_and(row_second == col_second, live)


def halves(x):
    lane = lax.broadcasted_iota(jnp.int32, x.shape, 1)
    zero = jnp.zeros_like(x)
    return jnp.where(lane < HEAD_DIM, x, zero), jnp.where(lane < HEAD_DIM, zero, x)


def kinds(lengths):
    row = lax.broadcasted_iota(jnp.int32, (ROWS, 1), 0)
    second = jnp.logical_and(row >= BUCKET, lengths[1] > 0).astype(jnp.int32)
    length = jnp.where(second == 1, lengths[1], lengths[0])
    return (row - BUCKET * second >= length // 2).astype(jnp.float32)


EMB_G, EMB_B, MLM_B, MLM_G, MLM_LB, TYPE_ZERO, TYPE_ONE = range(7)


def forward_kernel(
    lengths,
    found,
    place,
    lift,
    wide,
    tall,
    vec,
    final,
    embed_hat,
    embed_inverse,
    normed_half,
    rights,
    projected,
    weighting,
    hat_one,
    inverse_one,
    slope,
    active,
    hat_two,
    inverse_two,
    hidden,
):
    layer = pl.program_id(0)

    def row(index):
        return wide_row(vec, index)

    @pl.when(layer == 0)
    def _():
        two = (lengths[1] > 0).astype(jnp.float32)
        kind = kinds(lengths)
        lower = place[pl.ds(BUCKET, BUCKET), :]
        lower = jnp.where(two > 0, place[pl.ds(0, BUCKET), :], lower)
        embedded = found[...] + jnp.concatenate([place[pl.ds(0, BUCKET), :], lower], 0)
        zero, one = short_row(vec, TYPE_ZERO), short_row(vec, TYPE_ONE)
        hat, inverse = norm_forward(embedded + jnp.where(kind > 0, one, zero))
        embed_hat[...] = hat
        embed_inverse[...] = inverse
        normed = to_half(hat * short_row(vec, EMB_G) + short_row(vec, EMB_B))
        normed_half[...] = normed
        hidden[...] = nn(normed, lift[...]) + row(PROJ_B)

    half = to_half(hidden[...])
    rights[0] = half
    for part, bias in ((0, Q_B), (1, None), (2, V_B)):
        for low in range(0, D, 256):
            here = part * D + low
            value = nt(half, wide[pl.ds(here, 256), :])
            if bias is not None:
                value = value + lanes_of(vec, (bias * D + low) // 128, 2)
            projected[:, pl.ds(here, 256)] = to_half(value)
    allowed = allowed_block(lengths)
    for pair in range(HEADS // 2):
        lanes = pair * PAIR
        queries = halves(projected[:, pl.ds(lanes, PAIR)])
        keys = projected[:, pl.ds(D + lanes, PAIR)]
        values = halves(projected[:, pl.ds(2 * D + lanes, PAIR)])
        total = jnp.zeros((ROWS, PAIR), jnp.float32)
        for side in (0, 1):
            scores = jnp.where(allowed, nt(queries[side], keys) * SCALE, MASKED)
            powers = jnp.exp(scores - jnp.max(scores, -1, keepdims=True))
            weights = powers * (1.0 / jnp.sum(powers, -1, keepdims=True))
            weighting[2 * pair + side] = weights
            total = total + nn(to_half(weights), values[side])
        rights[1, :, pl.ds(lanes, PAIR)] = to_half(total)
    first_sum = hidden[...] + nt(rights[1], wide[pl.ds(3 * D, D), :]) + row(O_B)
    hat, inverse = norm_forward(first_sum)
    hat_one[...] = hat
    inverse_one[...] = inverse
    middle = hat * row(LN1_G) + row(LN1_B)
    half = to_half(middle)
    rights[2] = half
    total = middle + row(FFO_B)
    for low in range(0, FF, CHUNK):
        bias = lanes_of(vec, FF_AT + low // 128, CHUNK // 128)
        inner = nt(half, wide[pl.ds(4 * D + low, CHUNK), :]) + bias
        square = inner * inner
        bend = jnp.tanh(GELU_A * inner * (1.0 + GELU_B * square))
        act = to_half(0.5 * inner * (1.0 + bend))
        slope[:, pl.ds(low, CHUNK)] = 0.5 * (1.0 + bend) + (0.5 * GELU_A) * inner * (
            1.0 - bend * bend
        ) * (1.0 + 3.0 * GELU_B * square)
        active[pl.ds(low, CHUNK), :] = act.T
        total = total + nn(act, tall[pl.ds(low, CHUNK), :])
    hat, inverse = norm_forward(total)
    hat_two[...] = hat
    inverse_two[...] = inverse
    output = hat * row(LN2_G) + row(LN2_B)
    hidden[...] = output
    final[...] = output


def whole_spec():
    return pl.BlockSpec(memory_space=VMEM_SPACE, pipeline_mode=pl.Buffered(1))


def lift_spec():
    return pl.BlockSpec((E, D), lambda i: ((E + D) // E, 0), pipeline_mode=pl.Buffered(1))


def by_layer(*shape, order=lambda i: i):
    return pl.BlockSpec(
        (None, *shape), lambda i: (order(i),) + (0,) * len(shape), memory_space=VMEM_SPACE
    )


def run_forward(lengths, found, place, head, wide, tall, vec):
    def kept(*shape, dtype=jnp.bfloat16):
        return jax.ShapeDtypeStruct((LAYERS, *shape), dtype)

    single = jnp.float32
    names = (
        "final",
        "embed_hat",
        "embed_inverse",
        "normed_half",
        "rights",
        "projected",
        "weighting",
        "hat_one",
        "inverse_one",
        "slope",
        "active",
        "hat_two",
        "inverse_two",
    )
    outs = pl.pallas_call(
        forward_kernel,
        grid=(LAYERS,),
        out_shape=[
            jax.ShapeDtypeStruct((ROWS, D), single),
            jax.ShapeDtypeStruct((ROWS, E), single),
            jax.ShapeDtypeStruct((ROWS, 1), single),
            jax.ShapeDtypeStruct((ROWS, E), jnp.bfloat16),
            jax.ShapeDtypeStruct((3, LAYERS, ROWS, D), jnp.bfloat16),
            kept(ROWS, 3 * D),
            kept(HEADS, ROWS, ROWS, dtype=single),
            kept(ROWS, D, dtype=single),
            kept(ROWS, 1, dtype=single),
            kept(ROWS, FF, dtype=single),
            jax.ShapeDtypeStruct((FF, LAYERS * ROWS), jnp.bfloat16),
            kept(ROWS, D, dtype=single),
            kept(ROWS, 1, dtype=single),
        ],
        in_specs=[pl.BlockSpec(memory_space=pltpu.SMEM)]
        + [whole_spec()] * 2
        + [lift_spec()]
        + [whole_spec()] * 3,
        out_specs=[
            pl.BlockSpec((ROWS, D), lambda i: (0, 0)),
            pl.BlockSpec((ROWS, E), lambda i: (0, 0)),
            pl.BlockSpec((ROWS, 1), lambda i: (0, 0)),
            pl.BlockSpec((ROWS, E), lambda i: (0, 0)),
            pl.BlockSpec((3, None, ROWS, D), lambda i: (0, i, 0, 0)),
            by_layer(ROWS, 3 * D),
            by_layer(HEADS, ROWS, ROWS),
            by_layer(ROWS, D),
            by_layer(ROWS, 1),
            by_layer(ROWS, FF),
            pl.BlockSpec((FF, ROWS), lambda i: (0, i)),
            by_layer(ROWS, D),
            by_layer(ROWS, 1),
        ],
        scratch_shapes=[VMEM_SPACE((ROWS, D), single)],
        compiler_params=pltpu.CompilerParams(
            dimension_semantics=("arbitrary",), vmem_limit_bytes=VMEM_ASK
        ),
    )(lengths, found, place, head, wide, tall, vec)
    return dict(zip(names, outs))


def backward_kernel(
    lengths,
    start,
    wide_sums,
    small_sums,
    embed_hat,
    embed_inverse,
    normed_half,
    lift,
    head_in,
    wide,
    tall,
    vec,
    projected,
    weighting,
    hat_one,
    inverse_one,
    slope,
    hat_two,
    inverse_two,
    rows_out,
    back_lift,
    turned,
    outer,
    vector,
    sums,
    ff_sum,
    upstream,
    back_mixed,
    joint,
):
    step = pl.program_id(0)

    @pl.when(step == 0)
    def _():
        upstream[...] = start[...]
        sums[...] = jnp.zeros_like(sums)
        ff_sum[...] = jnp.zeros_like(ff_sum)

    def row(index):
        return wide_row(vec, index)

    def add_sum(index, value):
        here = pl.ds(index - Q_B, 1)
        sums[here, :] = sums[here, :] + jnp.sum(value, 0, keepdims=True)

    up = upstream[...]
    hat = hat_two[...]
    add_sum(LN2_G, up * hat)
    add_sum(LN2_B, up)
    back_second = norm_backward(up, row(LN2_G), hat, inverse_two[...])
    half = to_half(back_second)
    outer[...] = half
    add_sum(FFO_B, half.astype(jnp.float32))
    total = back_second
    for low in range(0, FF, CHUNK):
        lanes = pl.ds(low, CHUNK)
        inner = to_half(nt(half, tall[lanes, :]) * slope[:, lanes])
        ff_sum[:, lanes] = ff_sum[:, lanes] + jnp.sum(
            inner.astype(jnp.float32), 0, keepdims=True
        )
        turned[pl.ds(4 * D + low, CHUNK), :] = inner.T
        total = total + nn(inner, wide[pl.ds(4 * D + low, CHUNK), :])
    hat = hat_one[...]
    add_sum(LN1_G, total * hat)
    add_sum(LN1_B, total)
    back_first = norm_backward(total, row(LN1_G), hat, inverse_one[...])
    upstream[...] = back_first
    half = to_half(back_first)
    add_sum(O_B, half.astype(jnp.float32))
    turned[pl.ds(3 * D, D), :] = half.T
    back_mixed[...] = to_half(nn(half, wide[pl.ds(3 * D, D), :]))
    for pair in range(HEADS // 2):
        lanes = pair * PAIR
        queries = halves(projected[:, pl.ds(lanes, PAIR)])
        keys = halves(projected[:, pl.ds(D + lanes, PAIR)])
        values = projected[:, pl.ds(2 * D + lanes, PAIR)]
        grads = halves(back_mixed[:, pl.ds(lanes, PAIR)])
        zero = jnp.zeros((ROWS, PAIR), jnp.float32)
        back_query, back_key, back_value = zero, zero, zero
        for side in (0, 1):
            weights = weighting[2 * pair + side]
            soft = nt(grads[side], values)
            scores = to_half(
                weights * (soft - jnp.sum(weights * soft, -1, keepdims=True))
            )
            back_query = back_query + nn(scores, keys[side])
            back_key = back_key + tn(scores, queries[side])
            back_value = back_value + tn(to_half(weights), grads[side])
        joint[:, pl.ds(lanes, PAIR)] = to_half(back_query * SCALE)
        joint[:, pl.ds(D + lanes, PAIR)] = to_half(back_key * SCALE)
        joint[:, pl.ds(2 * D + lanes, PAIR)] = to_half(back_value)
    total = upstream[...]
    for part, bias in ((0, Q_B), (1, None), (2, V_B)):
        here = pl.ds(part * D, D)
        value = joint[:, here]
        if bias is not None:
            add_sum(bias, value.astype(jnp.float32))
        turned[here, :] = value.T
        total = total + nn(value, wide[here, :])
    upstream[...] = total

    @pl.when(step == LAYERS - 1)
    def _():
        half = to_half(upstream[...])
        back_lift[...] = to_half(tn(normed_half[...], half))
        back_normed = nt(half, lift[...])
        hat = embed_hat[...]
        back = norm_backward(back_normed, short_row(vec, EMB_G), hat, embed_inverse[...])
        rows_out[...] = to_half(back)
        kind = kinds(lengths)
        ones = jnp.sum(back * kind, 0, keepdims=True)
        zeros = jnp.sum(back * (1.0 - kind), 0, keepdims=True)
        vector[...] = jnp.zeros_like(vector)
        parts = [jnp.sum(half.astype(jnp.float32), 0, keepdims=True)]
        parts += [sums[pl.ds(i, 1), :] for i in range(8)]
        parts += [wide_sums[pl.ds(i, 1), :] for i in range(3)]
        parts += [ff_sum[...]]
        parts += [
            jnp.sum(back_normed * hat, 0, keepdims=True),
            jnp.sum(back_normed, 0, keepdims=True),
        ]
        parts += [small_sums[pl.ds(i, 1), :] for i in range(3)]
        parts += [zeros, ones]
        at = 0
        for part in parts:
            for low in range(0, part.shape[1], 128):
                vector[pl.ds(at, 1), :] = part[:, low : low + 128]
                at += 1


def run_backward(lengths, start, wide_sums, small_sums, head, back_head, wide, tall, vec, kept, lines):
    single, half = jnp.float32, jnp.bfloat16
    last = LAYERS - 1

    def order(i):
        return last - i

    return pl.pallas_call(
        backward_kernel,
        grid=(LAYERS,),
        out_shape=[
            jax.ShapeDtypeStruct((ROWS, E), half),
            jax.ShapeDtypeStruct(back_head.shape, half),
            jax.ShapeDtypeStruct((4 * D + FF, LAYERS * ROWS), half),
            jax.ShapeDtypeStruct((LAYERS, ROWS, D), half),
            jax.ShapeDtypeStruct((lines, 128), single),
        ],
        in_specs=[pl.BlockSpec(memory_space=pltpu.SMEM)]
        + [whole_spec()] * 6
        + [lift_spec(), pl.BlockSpec(memory_space=pl.ANY)]
        + [whole_spec()] * 3
        + [
            by_layer(ROWS, 3 * D, order=order),
            by_layer(HEADS, ROWS, ROWS, order=order),
            by_layer(ROWS, D, order=order),
            by_layer(ROWS, 1, order=order),
            by_layer(ROWS, FF, order=order),
            by_layer(ROWS, D, order=order),
            by_layer(ROWS, 1, order=order),
        ],
        out_specs=[
            pl.BlockSpec((ROWS, E), lambda i: (0, 0)),
            pl.BlockSpec((E, D), lambda i: ((E + D) // E, 0)),
            pl.BlockSpec((4 * D + FF, ROWS), lambda i: (0, order(i))),
            by_layer(ROWS, D, order=order),
            pl.BlockSpec((lines, 128), lambda i: (0, 0)),
        ],
        input_output_aliases={8: 1},
        scratch_shapes=[
            VMEM_SPACE((8, D), single),
            VMEM_SPACE((1, FF), single),
            VMEM_SPACE((ROWS, D), single),
            VMEM_SPACE((ROWS, D), half),
            VMEM_SPACE((ROWS, 3 * D), half),
        ],
        compiler_params=pltpu.CompilerParams(
            dimension_semantics=("arbitrary",), vmem_limit_bytes=VMEM_ASK
        ),
    )(
        lengths,
        start,
        wide_sums,
        small_sums,
        kept["embed_hat"],
        kept["embed_inverse"],
        kept["normed_half"],
        head,
        back_head,
        wide,
        tall,
        vec,
        kept["projected"],
        kept["weighting"],
        kept["hat_one"],
        kept["inverse_one"],
        kept["slope"],
        kept["hat_two"],
        kept["inverse_two"],
    )


def local(
    mesh,
    word_table,
    position_table,
    head_weights,
    decoder_bias,
    layer_wide,
    layer_tall,
    vectors,
    word_first,
    word_second,
    position_first,
    position_second,
    head_first,
    head_second,
    decoder_first,
    decoder_second,
    wide_first,
    wide_second,
    tall_first,
    tall_second,
    vector_first,
    vector_second,
    token_ids,
    seq_lengths,
    mlm_rows,
    mlm_labels,
    sop_labels,
):
    network = Network(mesh)

    def fill(count, value):
        return jnp.full((count,), value, jnp.int32)

    slots = mlm_labels.shape[0]
    facts = jnp.concatenate(
        [
            token_ids,
            mlm_labels,
            fill(128 - slots, -1),
            mlm_rows,
            fill(128 - slots, -1),
            seq_lengths,
            sop_labels,
            fill(3 * 128 + 124, 0),
        ]
    ).reshape(8, 128)
    (wide, tall, head), all_facts, place, found = network.start(
        (layer_wide.T, layer_tall, head_weights.T), word_table, facts, position_table
    )
    devices = all_facts.shape[0]
    place = place.reshape(-1, E)
    vec = vectors.reshape(-1, 128)
    kept = run_forward(seq_lengths, found, place, head, wide, tall, vec)
    (back_final, back_word_head, back_decoder, back_head, wide_sums, small_sums, totals) = (
        network.head(
            seq_lengths,
            sop_labels,
            kept["final"],
            head,
            word_table,
            decoder_bias,
            all_facts,
            facts,
            vec,
        )
    )
    mlm_count, sop_count = totals[0, 3], totals[0, 4]
    total = vectors.shape[0]
    share = -(-total // (devices * 1024)) * 1024
    back_rows, back_head, turned, outer, vector_grad = run_backward(
        seq_lengths,
        back_final,
        wide_sums,
        small_sums,
        head,
        back_head,
        wide,
        tall,
        vec,
        kept,
        devices * share // 128,
    )
    sums, heights, back_word, back_place, last, ends = network.finish(
        turned,
        kept["active"],
        kept["rights"].reshape(3, -1, D),
        outer.reshape(-1, D),
        back_head,
        back_rows,
        vector_grad.reshape(devices, -1, 128),
        all_facts,
        back_word_head,
        back_decoder,
        totals,
        position_table.shape[0],
    )
    wide_at, tall_at, head_at = 0, heights[0], heights[0] + heights[1]

    def turned_group(weight, first, second, low):
        return (weight.T, first.T, second.T, sums, low, LEARN_RATE)

    def flat(x):
        return x[None]

    def lines(x):
        return x.reshape(-1, 128)

    groups = (
        (word_table, word_first, word_second, back_word, 0, LEARN_RATE),
        turned_group(layer_wide, wide_first, wide_second, wide_at),
        (layer_tall, tall_first, tall_second, sums, tall_at, LEARN_RATE),
        turned_group(head_weights, head_first, head_second, head_at),
        (position_table, position_first, position_second, back_place, None, LEARN_RATE),
        (flat(decoder_bias), flat(decoder_first), flat(decoder_second), back_decoder, None)
        + (LEARN_RATE,),
        (lines(vectors), lines(vector_first), lines(vector_second), last, None, SMALL_RATE),
    )
    word, wide, tall, head, position, decoder, vector = network.adam(ends, groups)

    def turn(arrays):
        return [x.T for x in arrays]

    def plain(arrays):
        return [x.reshape(-1) for x in arrays]

    updates = (*word, *position, *turn(head), *plain(decoder), *turn(wide), *tall, *plain(vector))
    grad_norm, mlm_sum, sop_total = ends[0, 0], ends[2, 0], ends[3, 0]
    return (*updates, mlm_sum, mlm_count, sop_total, sop_count, grad_norm)


def solution(mesh):
    rows = P(AXES, None)
    columns = P(None, AXES)
    flat = P(AXES)
    whole = P()
    return jax.shard_map(
        functools.partial(local, mesh),
        mesh=mesh,
        in_specs=(rows, rows, columns, flat, columns, rows, whole)
        + (rows, rows) * 2
        + (columns, columns, flat, flat, columns, columns, rows, rows, whole, whole)
        + (flat,) * 5,
        out_specs=(rows,) * 6
        + (columns,) * 3
        + (flat,) * 3
        + (columns,) * 3
        + (rows,) * 3
        + (whole,) * 8,
        check_vma=False,
    )
```

profile of v0, /device:TPU:0, one launch (start us, length us, event | category | flops | bytes accessed | tf_op | source)
XLA Modules:
  0.0 334.2 jit_solution(2929016691956497184)
XLA Ops:
  0.7 1.4 concatenate.3
  2.1 87.4 %shard_map.449 = (bf16[4,4,2,192,768]{4,3,2,1,0:T(8,128)(2,1)}, bf16[4,4,2,96,768]{4,3,2,1,0:T(8,128)(2,1)}, bf16[4,4,2,32,768]{4,3,2,1,0:T(8,128)(2,1)}, s32[4,...) custom-call(f32[192,768]{1,0:T(8,128)} %bitcast.48, f32[96,768]{1,0:T(8,128)} %refs_9_.1, ...), custom_call_target="tpu_custom_call" | custom-call | tf_op jit(solution)/shard_map/pallas_call | solution.py:467
  89.5 46.1 %shard_map.450 = (f32[256,768]{1,0:T(8,128)}, f32[256,128]{1,0:T(8,128)}, f32[256,1]{1,0:T(8,128)}, bf16[256,128]{1,0:T(8,128)(2,1)}, bf16[3,4,256,768]{3,2,1,0:...) custom-call(s32[2]{0:T(128)} %lengths.5, ...), custom_call_target="tpu_custom_call" | custom-call | tf_op jit(solution)/shard_map/pallas_call | solution.py:1814
  135.6 45.9 %shard_map.451 = (f32[256,768]{1,0:T(8,128)}, f32[960,128]{1,0:T(8,128)}, f32[1,960]{1,0:T(1,128)}, bf16[1024,768]{1,0:T(8,128)(2,1)}, f32[3,768]{1,0:T(4,128)}, /*index=5*/f32[3,128]{1,0:T(4,128)}, f32[1,128]{1,0:T(1,128)}) custom-call(s32[2]{0:T(128)} %lengths.5, s32[2]{0:T(128)} %sop_labels.1, f32[256,768]{1,0:T(8,128)} %get-tuple-element.88.final, ...), custom_call_target="tpu_custom_call" | custom-call | tf_op jit(solution)/shard_map/pallas_call | solution.py:1345
  181.5 46.0 %shard_map.452 = (bf16[256,128]{1,0:T(8,128)(2,1)}, bf16[1024,768]{1,0:T(8,128)(2,1)}, bf16[6144,1024]{1,0:T(8,128)(2,1)}, bf16[4,256,768]{2,1,0:T(8,128)(2,1)}, f32[256,128]{1,0:T(8,128)}) custom-call(s32[2]{0:T(128)} %lengths.5, f32[256,768]{1,0:T(8,128)} %get-tuple-element.90.start, ...), custom_call_target="tpu_custom_call", output_to_operand_aliasing={{1}: (8, {})} | custom-call | tf_op jit(solution)/shard_map/pallas_call | solution.py:1997
  227.6 0.0 copy-start
  227.6 97.8 %shard_map.453 = (f32[320,768]{1,0:T(8,128)}, f32[960,128]{1,0:T(8,128)}, f32[16,128]{1,0:T(8,128)}, f32[4,8,16,128]{3,2,1,0:T(8,128)}, f32[8,128]{1,0:T(8,128)}) custom-call(bf16[6144,1024]{1,0:T(8,128)(2,1)} %get-tuple-element.104.left_wide, bf16[3072,1024]{1,0:T(8,128)(2,1)} %get-tuple-element.105.left_tall, bf16[3,1024,768]{2,1,0:T(8,128)(2,1)} %bitcast.47, ...), custom_call_target="tpu_custom_call" | custom-call | tf_op jit(solution)/shard_map/pallas_call | solution.py:1028
  325.4 0.0 copy-done
  325.4 0.6 fusion.1
  326.0 1.3 fusion
  327.3 6.7 %shard_map.454 = (f32[960,128]{1,0:T(8,128)}, f32[960,128]{1,0:T(8,128)}, f32[960,128]{1,0:T(8,128)}, f32[192,768]{1,0:T(8,128)}, f32[192,768]{1,0:T(8,128)}, /*...) custom-call(f32[8,128]{1,0:T(8,128)} %get-tuple-element.114.refs_0_,, ...), custom_call_target="tpu_custom_call" | custom-call | tf_op jit(solution)/shard_map/pallas_call | solution.py:1434
  (2 shorter events, 0.0 us)
Async XLA Ops:
  227.6 97.8 %copy-start = (f32[1,128]{1,0:T(1,128)S(1)}, f32[1,128]{1,0:T(1,128)}, u32[]{:S(2)}) copy-start(f32[1,128]{1,0:T(1,128)} %get-tuple-element.113.totals) | copy-start | bytes 1540
where the time goes:
time: 335 us; the launch traced here: 334 us
  Pallas kernels  330 us (99%)
    pallas_call x1, Pallas kernels, run_finish(): pl.pallas_call(functools.partial(finish_kernel, planes, heights, split),...  97.8 us
    pallas_call x1, Pallas kernels, run_start(): pl.pallas_call(functools.partial(start_kernel, planes, rows, tuple(member...  87.4 us
    pallas_call x1, Pallas kernels, run_forward(): pl.pallas_call(forward_kernel, grid=(LAYERS,), out_shape=[jax.ShapeDtypeS...  46.1 us
    pallas_call x1, Pallas kernels, run_backward(): pl.pallas_call(backward_kernel, grid=(LAYERS,), out_shape=[jax.ShapeDtype...  46 us
    pallas_call x1, Pallas kernels, run_head(): pl.pallas_call(functools.partial(head_kernel, planes), out_shape=[jax.Sha...  45.9 us

commit v1 on v0

--- a/solution.py
+++ b/solution.py
@@ -114,10 +114,13 @@
 OWN, ACROSS_X, ACROSS_Y, DIAGONAL = 0, 1, 2, 3
 
 
-def cuts_of(rows):
-    tail = max(32, round(rows * 0.22 / 32) * 32)
+def cuts_of(rows, share):
+    tail = max(32, round(rows * share / 32) * 32)
     head = rows - tail
     return ((0, head), (head, rows))
+
+
+GATHER_TAIL, FINISH_TAIL = 0.3, 0.2
 
 
 def half_of(span, which):
@@ -138,7 +141,7 @@
 def gather_stages(planes, rows, members, x, outs, buf, sems, where, opening):
     out_sem, send, recv, side_send, side_recv = sems
     z, c, cols = where
-    cuts = cuts_of(rows)
+    cuts = cuts_of(rows, GATHER_TAIL)
     at_x, at_y, mate = (z, cols[1] * 2 + c), (z, cols[2] * 2 + c), (z, cols[0] * 2 + 1 - c)
     above, below = z < planes - 1, z > 0
     up, down = (z + 1, cols[0] * 2 + c), (z - 1, cols[0] * 2 + c)
@@ -377,8 +380,12 @@
     own_tall,
     own_head,
     own_word,
-    own_facts,
     own_place,
+    ids,
+    labels,
+    slot_rows,
+    lengths,
+    sop_labels,
     *refs,
 ):
     width = 8
@@ -393,8 +400,23 @@
     f = cols[0] * 2 + c
     line = [(lax.rem(z + d, planes), f) for d in range(1, planes)]
     plane = [(z, lax.rem(f + d, width)) for d in range(1, width)]
-    facts[z, f] = own_facts[...]
-    place[z, f] = to_half(own_place[...]).astype(jnp.float32)
+    lane = lax.broadcasted_iota(jnp.int32, (1, 128), 1)
+    rest = jnp.full((1, 128 - labels.shape[1]), -1, jnp.int32)
+    note = jnp.zeros((1, 128), jnp.int32)
+    for at, value in enumerate((lengths[0], lengths[1], sop_labels[0], sop_labels[1])):
+        note = note + jnp.where(lane == at, value, 0)
+    facts[z, f] = jnp.concatenate(
+        [
+            ids[:, :128],
+            ids[:, 128:],
+            jnp.concatenate([labels[...], rest], 1),
+            jnp.concatenate([slot_rows[...], rest], 1),
+            note,
+            jnp.zeros((3, 128), jnp.int32),
+        ],
+        0,
+    )
+    place[z, f] = to_half(own_place[...])
     greet([(None, who) for who in line + plane])
     pairs = (facts, place)
 
@@ -451,7 +473,7 @@
     return (z, cols[0] * 2 + 1 - c)
 
 
-def run_start(shards, own_word, own_facts, own_place, mesh_shape, identity):
+def run_start(shards, own_word, own_place, batch, mesh_shape, identity):
     planes, width = mesh_shape
     heights = tuple(shard.shape[0] for shard in shards)
     rows, columns = sum(heights), shards[1].shape[1]
@@ -471,11 +493,11 @@
             for height in heights
         ]
         + [
-            jax.ShapeDtypeStruct((planes, width, *own_facts.shape), own_facts.dtype),
-            jax.ShapeDtypeStruct((planes, width, *own_place.shape), own_place.dtype),
+            jax.ShapeDtypeStruct((planes, width, 8, 128), jnp.int32),
+            jax.ShapeDtypeStruct((planes, width, *own_place.shape), half),
             jax.ShapeDtypeStruct((ROWS, features), single),
         ],
-        in_specs=[vmem] * 6,
+        in_specs=[vmem] * 8 + [pl.BlockSpec(memory_space=pltpu.SMEM)] * 2,
         out_specs=[pl.BlockSpec(memory_space=pl.ANY)] * len(heights) + [vmem] * 3,
         scratch_shapes=[
             VMEM_SPACE((rows, columns), half),
@@ -501,12 +523,12 @@
         compiler_params=pltpu.CompilerParams(
             collective_id=identity, has_side_effects=True, vmem_limit_bytes=VMEM_ASK
         ),
-    )(*shards, own_word, own_facts, own_place)
+    )(*shards, own_word, own_place, *[x[None] for x in batch[:3]], *batch[3:])
     weights = [out.reshape(-1, columns) for out in outs]
     devices = planes * width
     return (
         weights,
-        facts.reshape(devices, *own_facts.shape),
+        facts.reshape(devices, 8, 128),
         place.reshape(devices, *own_place.shape),
         found,
     )
@@ -527,6 +549,7 @@
 
 
 ROWS_AT = 1
+TURN_AT = 5
 MATE_AT = 9
 
 
@@ -544,8 +567,8 @@
     split,
     left_wide,
     left_tall,
-    rights,
-    outer,
+    rights_from,
+    outer_from,
     head_grad,
     own_rows,
     vector_terms,
@@ -586,15 +609,24 @@
     vec_recv,
     end_send,
     end_recv,
+    rights,
+    outer,
+    right_load,
 ):
     width = 8
+    right_copies = [
+        pltpu.make_async_copy(rights_from.at[i], rights.at[i], right_load.at[i]) for i in range(3)
+    ]
+    right_copies.append(pltpu.make_async_copy(outer_from, outer, right_load.at[3]))
+    for copy in right_copies:
+        copy.start()
     wide_height, tall_height, head_height = heights
     rows = wide_height + tall_height + head_height
     z, c, cols = places()
     q = cols[0]
     f = q * 2 + c
     x, y = lax.rem(q, 2), q // 2
-    cuts = cuts_of(rows)
+    cuts = cuts_of(rows, FINISH_TAIL)
     head, tail = cuts
     head_rows, tail_rows = head[1] - head[0], tail[1] - tail[0]
     at_x, at_y, mate = (z, cols[1] * 2 + c), (z, cols[2] * 2 + c), (z, q * 2 + 1 - c)
@@ -667,6 +699,11 @@
             (z, cols[col] * 2 + c),
         )
 
+    def row_turn(which):
+        col, who = ((ACROSS_Y, at_x), (ACROSS_X, at_y))[which]
+        here = all_rows.at[:, cols[col], c, pl.ds(which * BUCKET, BUCKET)]
+        return remote(here, here, row_send.at[2, 1 + which], row_recv.at[2, 1 + which], who)
+
     def row_mate():
         return remote(
             all_rows.at[:, :, c], all_rows.at[:, :, c], row_send.at[2, 0], row_recv.at[2, 0], mate
@@ -750,14 +787,22 @@
             target = piece(both.at[zt, col, c], tail)
             accumulate(target, [target, tail_line.at[way, zt, col]], tail_rows)
 
-    def onward(zt, add, message):
-        for way, valid in ((0, zt > z), (1, zt < z)):
-            behind = (below, above)[way]
-            pl.when(jnp.logical_and(valid, behind))(functools.partial(add, zt, way))
-            pl.when(valid)(lambda way=way: message(zt, way).start())
-
-    def tail_step(zt):
-        onward(zt, tail_add, tail_message)
+    def ways(zt):
+        return ((0, zt > z, below), (1, zt < z, above))
+
+    def tail_open(zt):
+        for way, valid, behind in ways(zt):
+            go = jnp.logical_and(valid, jnp.logical_not(behind))
+            pl.when(go)(lambda way=way: tail_message(zt, way).start())
+
+    def tail_pass(zt):
+        for way, valid, behind in ways(zt):
+
+            def action(way=way):
+                tail_add(zt, way)
+                tail_message(zt, way).start()
+
+            pl.when(jnp.logical_and(valid, behind))(action)
 
     def line_add(zt, way):
         line_message(zt, way).wait_recv()
@@ -769,7 +814,18 @@
             full_message(zt, which).wait_recv()
         base = [piece(both.at[zt, OWN, c], head), full_in.at[0, zt], full_in.at[1, zt]]
         accumulate(base[0], base, head_rows)
-        onward(zt, line_add, line_message)
+        for way, valid, behind in ways(zt):
+            go = jnp.logical_and(valid, jnp.logical_not(behind))
+            pl.when(go)(lambda way=way: line_message(zt, way).start())
+
+    def line_pass(zt):
+        for way, valid, behind in ways(zt):
+
+            def action(way=way):
+                line_add(zt, way)
+                line_message(zt, way).start()
+
+            pl.when(jnp.logical_and(valid, behind))(action)
 
     def after(n):
         i, col = turn_of(n)
@@ -784,16 +840,35 @@
         @pl.when(col == OWN)
         def _():
             second(zt)
-            pl.when(i < planes - 1)(lambda: tail_step(zt))
+            pl.when(i < planes - 1)(lambda: tail_open(zt))
+            pl.when(i > 0)(lambda: tail_pass(plane_at(i - 1)))
             pl.when(i > 0)(lambda: third(plane_at(i - 1)))
-
-    for copy in head_copies:
+            pl.when(i > 1)(lambda: line_pass(plane_at(i - 2)))
+
+    for copy in head_copies + right_copies:
         copy.wait()
 
-    def await_plane_rows():
-        for step in (ACROSS_X, ACROSS_Y, DIAGONAL):
+    def turn_rows():
+        for step in (ACROSS_X, ACROSS_Y):
             here = all_rows.at[:, cols[step], c]
             remote(here, here, row_send.at[1, step], row_recv.at[1, step], mate).wait_recv()
+        for which in (0, 1):
+            row_turn(which).start()
+
+    def share_rows():
+        for which in (0, 1):
+            here = all_rows.at[:, cols[DIAGONAL], c, pl.ds(which * BUCKET, BUCKET)]
+            remote(
+                here, here, row_send.at[2, 1 + which], row_recv.at[2, 1 + which], mate
+            ).wait_recv()
+        row_mate().start()
+
+    def sum_vector():
+        total = vector_mid[z]
+        for d, who in enumerate(line):
+            vector_second(d, who).wait_recv()
+            total = total + vector_last[d]
+        last[z, f, 0:8] = total
 
     def body(n, unused):
         for copy in fetches(n):
@@ -821,7 +896,7 @@
         def _():
             for d, who in enumerate(line):
                 row_line(d, who).wait_recv()
-            for step in (ACROSS_X, ACROSS_Y, DIAGONAL):
+            for step in (ACROSS_X, ACROSS_Y):
                 row_plane(step).start()
             total = vector_terms[:, f]
             for d, who in enumerate(plane):
@@ -831,15 +906,15 @@
             for d, who in enumerate(line):
                 vector_second(d, who).start()
 
-        @pl.when(n == MATE_AT)
-        def _():
-            await_plane_rows()
-            row_mate().start()
+        pl.when(n == TURN_AT)(turn_rows)
+        pl.when(n == MATE_AT)(share_rows)
 
         return unused
 
     lax.fori_loop(0, 4 * planes, body, 0)
     after(jnp.int32(4 * planes - 1))
+    targets = [plane_at(i) for i in range(planes)]
+    sum_vector()
     here = all_rows.at[:, :, 1 - c]
     remote(here, here, row_send.at[2, 0], row_recv.at[2, 0], mate).wait_recv()
     words = word_grad.shape[0]
@@ -862,8 +937,6 @@
         lax.fori_loop(first, after, body, 0)
 
     word_grad[...] = base_word[...]
-    look_back(0, 2 * planes)
-    targets = [plane_at(i) for i in range(planes)]
 
     def tail_half_message(which):
         return remote(
@@ -887,7 +960,8 @@
     pl.when(above)(lambda: tail_add(z, 1))
     for which in (0, 1):
         push(None, functools.partial(tail_half_message, which))
-    look_back(2 * planes, 4 * planes)
+    line_pass(targets[planes - 2])
+    look_back(0, 4 * planes)
     for which, col in ((1, ACROSS_X), (0, ACROSS_Y)):
         tail_half_message(which).wait_recv()
         target = piece(both.at[z, col, c], half_of(tail, which))
@@ -914,10 +988,6 @@
         [piece(both.at[z, OWN, c], tail), tail_full.at[0], tail_full.at[1]],
         tail_rows,
     )
-    total = vector_mid[z]
-    for d, who in enumerate(line):
-        vector_second(d, who).wait_recv()
-        total = total + vector_last[d]
     height = place_grad.shape[0]
     own = z * width + f
     low_half = (own * height < BUCKET).astype(jnp.float32)
@@ -939,7 +1009,6 @@
     squares = jnp.sum(grad * grad) + jnp.sum(back_decoder[...] * back_decoder[...])
     squares = squares + jnp.sum(word_grad[...] * word_grad[...])
     squares = squares + jnp.sum(out[...] * out[...])
-    last[z, f, 0:8] = total
     last[z, f, 8:16] = jnp.concatenate(
         [totals[...], jnp.where(lane == 0, squares, 0.0), jnp.zeros((6, 128), jnp.float32)], 0
     )
@@ -964,9 +1033,13 @@
     norm = jnp.sqrt(jnp.broadcast_to(squares, (1, 128)))
     factor = jnp.minimum(1.0, CLIP_NORM / (norm + NORM_EPSILON))
     mlm = totals[0:1, :] - jnp.sum(jnp.where(lane == 1, tails[0:1, :], 0.0))
+    def count(at):
+        own = jnp.where(lane == at, totals[0:1, :], 0.0)
+        return jnp.broadcast_to(jnp.sum(own, 1, keepdims=True), (1, 128))
+
     sop = jnp.zeros((1, 128), jnp.float32) + jnp.sum(jnp.where(lane == 2, tails[0:1, :], 0.0))
     ends[...] = jnp.concatenate(
-        [norm, factor, mlm, sop, jnp.zeros((4, 128), jnp.float32)], 0
+        [norm, factor, mlm, sop, count(3), count(4), jnp.zeros((2, 128), jnp.float32)], 0
     )
     for copy in first_copies + second_copies:
         copy.wait_send()
@@ -986,8 +1059,10 @@
                 line_message(zt, way).wait_send()
 
             pl.when(valid)(done)
-    for step in (ACROSS_X, ACROSS_Y, DIAGONAL):
+    for step in (ACROSS_X, ACROSS_Y):
         row_plane(step).wait_send()
+    for which in (0, 1):
+        row_turn(which).wait_send()
     for d, who in enumerate(line):
         vector_second(d, who).wait_send()
 
@@ -1019,7 +1094,7 @@
     rows = sum(heights)
     long = left_wide.shape[1]
     split = (3 * D // (2 * heights[0]), 4 * D // (2 * heights[0]))
-    head, tail = (high - low for low, high in cuts_of(rows))
+    head, tail = (high - low for low, high in cuts_of(rows, FINISH_TAIL))
     half, single = jnp.bfloat16, jnp.float32
     block = vector_terms.shape[1:]
     vmem = pl.BlockSpec(memory_space=VMEM_SPACE)
@@ -1034,7 +1109,7 @@
             jax.ShapeDtypeStruct((planes, width, 16, 128), single),
             jax.ShapeDtypeStruct((8, 128), single),
         ],
-        in_specs=[any_space, any_space, vmem, vmem, any_space, vmem, vmem] + [vmem] * 4,
+        in_specs=[any_space] * 5 + [vmem] * 6,
         out_specs=[vmem] * 5,
         scratch_shapes=[
             VMEM_SPACE((planes, width // 2, 2, *own_rows.shape), half),
@@ -1065,6 +1140,9 @@
             dma((2, width)),
             dma((2, width)),
             dma((2, width)),
+            VMEM_SPACE(rights.shape, half),
+            VMEM_SPACE(outer.shape, half),
+            dma((4,)),
         ],
         compiler_params=pltpu.CompilerParams(
             collective_id=identity, has_side_effects=True, vmem_limit_bytes=VMEM_ASK
@@ -1114,7 +1192,6 @@
     word,
     decoder,
     facts,
-    own_facts,
     vec,
     back_final,
     back_word,
@@ -1186,7 +1263,7 @@
 
     final_half = to_half(final[...])
     place = lax.broadcasted_iota(jnp.int32, (ROWS, LIFT), 0)
-    scatter = to_half((place == own_facts[3:4, :]).astype(single))
+    scatter = to_half((place == facts[z * width + f, 3:4, :]).astype(single))
     pick = scatter.T
     picked = to_half(nn(pick, final_half))
     dense = nt(picked, head[:E, :]) + short_row(vec, MLM_B)
@@ -1332,7 +1409,7 @@
 
 
 def run_head(
-    lengths, sop_labels, final, head, word, decoder, facts, own_facts, vec, mesh_shape, identity
+    lengths, sop_labels, final, head, word, decoder, facts, vec, mesh_shape, identity
 ):
     planes, width = mesh_shape
     words = word.shape[0]
@@ -1353,7 +1430,7 @@
             jax.ShapeDtypeStruct((3, E), single),
             jax.ShapeDtypeStruct((1, 128), single),
         ],
-        in_specs=[smem] * 2 + [vmem] * 7,
+        in_specs=[smem] * 2 + [vmem] * 6,
         out_specs=[vmem] * 7,
         scratch_shapes=[
             VMEM_SPACE((planes, width, WIRE, E), half),
@@ -1370,7 +1447,7 @@
         compiler_params=pltpu.CompilerParams(
             collective_id=identity, has_side_effects=True, vmem_limit_bytes=VMEM_ASK
         ),
-    )(lengths, sop_labels, final, head, word, decoder, facts, own_facts, vec)
+    )(lengths, sop_labels, final, head, word, decoder, facts, vec)
 
 
 def adam_update(weight, gradient, first, second, rate):
@@ -1387,7 +1464,7 @@
 def adam_kernel(blocks, rates, *refs):
     count = len(rates)
     ends, refs = refs[0], refs[1:]
-    ins, outs = refs[: 4 * count], refs[4 * count :]
+    ins, outs, scalars = refs[: 4 * count], refs[4 * count : 7 * count], refs[7 * count :]
     factor = ends[1:2, 0:1]
 
     def update(number):
@@ -1408,6 +1485,9 @@
     def _():
         for number in range(blocks, count):
             update(number)
+        lane = lax.broadcasted_iota(jnp.int32, (1, 128), 1)
+        for at, scalar in enumerate(scalars):
+            scalar[0] = jnp.sum(jnp.where(lane == 0, ends[at : at + 1, :], 0.0))
 
 
 def run_adam(ends, groups, steps):
@@ -1431,6 +1511,8 @@
         out_specs += [spec] * 3
         shapes += [jax.ShapeDtypeStruct(weight.shape, jnp.float32)] * 3
         given += [weight, first, second, gradient]
+    out_specs += [pl.BlockSpec(memory_space=pltpu.SMEM)] * 6
+    shapes += [jax.ShapeDtypeStruct((1,), jnp.float32)] * 6
     return pl.pallas_call(
         functools.partial(adam_kernel, blocks, tuple(group[5] for group in groups)),
         grid=(steps,),
@@ -1454,14 +1536,20 @@
         self.calls += 1
         return self.calls
 
-    def start(self, shards, own_word, own_facts, own_place):
+    def start(self, shards, own_word, own_place, batch):
         if self.kernels:
-            return run_start(
-                shards, own_word, own_facts, own_place, self.shape, self.identity()
-            )
+            return run_start(shards, own_word, own_place, batch, self.shape, self.identity())
+        token_ids, labels, slot_rows, lengths, sop_labels = batch
+
+        def fill(count, value):
+            return jnp.full((count,), value, jnp.int32)
+
+        rest = fill(128 - labels.shape[0], -1)
+        own_facts = [token_ids, labels, rest, slot_rows, rest, lengths, sop_labels]
+        own_facts = jnp.concatenate([*own_facts, fill(3 * 128 + 124, 0)]).reshape(8, 128)
         weights = [lax.all_gather(to_half(w), AXES, axis=0, tiled=True) for w in shards]
         facts = lax.all_gather(own_facts, AXES)
-        place = lax.all_gather(to_half(own_place), AXES).astype(jnp.float32)
+        place = lax.all_gather(to_half(own_place), AXES)
         words = own_word.shape[0]
         ids = facts[:, : ROWS // 128].reshape(-1) - lax.axis_index(AXES) * words
         column = jnp.arange(words, dtype=jnp.int32)
@@ -1470,14 +1558,14 @@
         found = lax.psum_scatter(terms, AXES, scatter_dimension=0, tiled=True)
         return weights, facts, place, found
 
-    def head(self, lengths, sop_labels, final, head, word, decoder, facts, own_facts, vec):
+    def head(self, lengths, sop_labels, final, head, word, decoder, facts, vec):
         decoder = decoder[None]
-        given = (lengths, sop_labels, final, head, word, decoder, facts, own_facts, vec)
+        given = (lengths, sop_labels, final, head, word, decoder, facts, vec)
         if self.kernels:
             return run_head(*given, self.shape, self.identity())
         return self.plain_head(*given)
 
-    def plain_head(self, lengths, sop_labels, final, head, word, decoder, facts, own_facts, vec):
+    def plain_head(self, lengths, sop_labels, final, head, word, decoder, facts, vec):
         short, cls = vec[SHORT_AT:], vec[CLS_AT:FF_AT].reshape(2, D)
         pool_b = vec[POOL_B * D // 128 : CLS_AT].reshape(D)
         labels = facts[:, 2, :WIRE].reshape(1, -1)
@@ -1486,7 +1574,7 @@
         single = jnp.float32
         offset = lax.axis_index(AXES) * word.shape[0]
         word_half, final_half = to_half(word), to_half(final)
-        rows = own_facts[3, :WIRE]
+        rows = facts[lax.axis_index(AXES), 3, :WIRE]
         pick = (rows[:, None] == jnp.arange(ROWS, dtype=jnp.int32)[None]).astype(single)
         picked = to_half(product(to_half(pick), final_half))
         dense = times_transpose(picked, head[:E]) + short[MLM_B]
@@ -1545,7 +1633,8 @@
     def adam(self, ends, groups):
         if self.kernels:
             updates = run_adam(ends, groups, 4)
-            return [updates[i : i + 3] for i in range(0, len(updates), 3)]
+            scalars = [x.reshape(()) for x in updates[-6:]]
+            return [updates[i : i + 3] for i in range(0, 3 * len(groups), 3)], scalars
         updates = []
         for weight, first, second, gradient, low, rate in groups:
             rows = weight.shape[0]
@@ -1553,7 +1642,7 @@
                 gradient = gradient[low : low + rows]
             gradient = gradient.reshape(-1, weight.shape[1])[:rows]
             updates.append(adam_update(weight, ends[1, 0] * gradient, first, second, rate))
-        return updates
+        return updates, [ends[i, 0] for i in range(6)]
 
     def finish(
         self,
@@ -1618,8 +1707,9 @@
         reduced, tails, squares = lax.psum((vector, totals, squares), AXES)
         norm = jnp.sqrt(squares + jnp.sum(reduced * reduced))
         factor = jnp.minimum(1.0, CLIP_NORM / (norm + NORM_EPSILON))
-        ends = jnp.stack([norm, factor, totals[0, 0] - tails[0, 1], tails[0, 2]])
-        ends = jnp.broadcast_to(ends[:, None], (4, 128))
+        ends = [norm, factor, totals[0, 0] - tails[0, 1], tails[0, 2]]
+        ends = jnp.stack([*ends, totals[0, 3], totals[0, 4]])
+        ends = jnp.broadcast_to(ends[:, None], (6, 128))
         heights = tuple(total.shape[0] for total in sums)
         return jnp.concatenate(sums, 0), heights, word_grad, place_grad, reduced, ends
 
@@ -1658,14 +1748,20 @@
 
 def allowed_block(lengths):
     shape = (ROWS, ROWS)
-    row = lax.broadcasted_iota(jnp.int32, shape, 0)
-    col = lax.broadcasted_iota(jnp.int32, shape, 1)
+    key = lax.broadcasted_iota(jnp.int32, shape, 0)
+    query = lax.broadcasted_iota(jnp.int32, shape, 1)
     two = lengths[1] > 0
-    row_second = jnp.logical_and(row >= BUCKET, two).astype(jnp.int32)
-    col_second = jnp.logical_and(col >= BUCKET, two).astype(jnp.int32)
-    length = jnp.where(col_second == 1, lengths[1], lengths[0])
-    live = col - BUCKET * col_second < length
-    return jnp.logical_and(row_second == col_second, live)
+    key_second = jnp.logical_and(key >= BUCKET, two).astype(jnp.int32)
+    query_second = jnp.logical_and(query >= BUCKET, two).astype(jnp.int32)
+    length = jnp.where(key_second == 1, lengths[1], lengths[0])
+    live = key - BUCKET * key_second < length
+    return jnp.logical_and(query_second == key_second, live)
+
+
+def halves_down(x):
+    row = lax.broadcasted_iota(jnp.int32, x.shape, 0)
+    zero = jnp.zeros_like(x)
+    return jnp.where(row < HEAD_DIM, x, zero), jnp.where(row < HEAD_DIM, zero, x)
 
 
 def halves(x):
@@ -1716,9 +1812,9 @@
     def _():
         two = (lengths[1] > 0).astype(jnp.float32)
         kind = kinds(lengths)
-        lower = place[pl.ds(BUCKET, BUCKET), :]
-        lower = jnp.where(two > 0, place[pl.ds(0, BUCKET), :], lower)
-        embedded = found[...] + jnp.concatenate([place[pl.ds(0, BUCKET), :], lower], 0)
+        upper = place[pl.ds(0, BUCKET), :].astype(jnp.float32)
+        lower = jnp.where(two > 0, upper, place[pl.ds(BUCKET, BUCKET), :].astype(jnp.float32))
+        embedded = found[...] + jnp.concatenate([upper, lower], 0)
         zero, one = short_row(vec, TYPE_ZERO), short_row(vec, TYPE_ONE)
         hat, inverse = norm_forward(embedded + jnp.where(kind > 0, one, zero))
         embed_hat[...] = hat
@@ -1741,15 +1837,15 @@
         lanes = pair * PAIR
         queries = halves(projected[:, pl.ds(lanes, PAIR)])
         keys = projected[:, pl.ds(D + lanes, PAIR)]
-        values = halves(projected[:, pl.ds(2 * D + lanes, PAIR)])
-        total = jnp.zeros((ROWS, PAIR), jnp.float32)
+        values = halves_down(projected[:, pl.ds(2 * D + lanes, PAIR)].T)
+        total = jnp.zeros((PAIR, ROWS), jnp.float32)
         for side in (0, 1):
-            scores = jnp.where(allowed, nt(queries[side], keys) * SCALE, MASKED)
-            powers = jnp.exp(scores - jnp.max(scores, -1, keepdims=True))
-            weights = powers * (1.0 / jnp.sum(powers, -1, keepdims=True))
+            scores = jnp.where(allowed, nt(keys, queries[side]) * SCALE, MASKED)
+            powers = jnp.exp(scores - jnp.max(scores, 0, keepdims=True))
+            weights = powers * (1.0 / jnp.sum(powers, 0, keepdims=True))
             weighting[2 * pair + side] = weights
-            total = total + nn(to_half(weights), values[side])
-        rights[1, :, pl.ds(lanes, PAIR)] = to_half(total)
+            total = total + nn(values[side], to_half(weights))
+        rights[1, :, pl.ds(lanes, PAIR)] = to_half(total).T
     first_sum = hidden[...] + nt(rights[1], wide[pl.ds(3 * D, D), :]) + row(O_B)
     hat, inverse = norm_forward(first_sum)
     hat_one[...] = hat
@@ -1931,30 +2027,32 @@
     for pair in range(HEADS // 2):
         lanes = pair * PAIR
         queries = halves(projected[:, pl.ds(lanes, PAIR)])
-        keys = halves(projected[:, pl.ds(D + lanes, PAIR)])
+        keys = halves_down(projected[:, pl.ds(D + lanes, PAIR)].T)
         values = projected[:, pl.ds(2 * D + lanes, PAIR)]
         grads = halves(back_mixed[:, pl.ds(lanes, PAIR)])
         zero = jnp.zeros((ROWS, PAIR), jnp.float32)
-        back_query, back_key, back_value = zero, zero, zero
+        back_query, back_key, back_value = jnp.zeros((PAIR, ROWS), jnp.float32), zero, zero
         for side in (0, 1):
             weights = weighting[2 * pair + side]
-            soft = nt(grads[side], values)
-            scores = to_half(
-                weights * (soft - jnp.sum(weights * soft, -1, keepdims=True))
-            )
-            back_query = back_query + nn(scores, keys[side])
-            back_key = back_key + tn(scores, queries[side])
-            back_value = back_value + tn(to_half(weights), grads[side])
-        joint[:, pl.ds(lanes, PAIR)] = to_half(back_query * SCALE)
-        joint[:, pl.ds(D + lanes, PAIR)] = to_half(back_key * SCALE)
-        joint[:, pl.ds(2 * D + lanes, PAIR)] = to_half(back_value)
+            soft = nt(values, grads[side])
+            scores = to_half(weights * (soft - jnp.sum(weights * soft, 0, keepdims=True)))
+            back_query = back_query + nn(keys[side], scores)
+            back_key = back_key + nn(scores, queries[side])
+            back_value = back_value + nn(to_half(weights), grads[side])
+        query_half = to_half(back_query * SCALE)
+        key_half, value_half = to_half(back_key * SCALE), to_half(back_value)
+        joint[:, pl.ds(lanes, PAIR)] = query_half.T
+        joint[:, pl.ds(D + lanes, PAIR)] = key_half
+        joint[:, pl.ds(2 * D + lanes, PAIR)] = value_half
+        turned[pl.ds(lanes, PAIR), :] = query_half
+        turned[pl.ds(D + lanes, PAIR), :] = key_half.T
+        turned[pl.ds(2 * D + lanes, PAIR), :] = value_half.T
     total = upstream[...]
     for part, bias in ((0, Q_B), (1, None), (2, V_B)):
         here = pl.ds(part * D, D)
         value = joint[:, here]
         if bias is not None:
             add_sum(bias, value.astype(jnp.float32))
-        turned[here, :] = value.T
         total = total + nn(value, wide[here, :])
     upstream[...] = total
 
@@ -2089,24 +2187,11 @@
 ):
     network = Network(mesh)
 
-    def fill(count, value):
-        return jnp.full((count,), value, jnp.int32)
-
-    slots = mlm_labels.shape[0]
-    facts = jnp.concatenate(
-        [
-            token_ids,
-            mlm_labels,
-            fill(128 - slots, -1),
-            mlm_rows,
-            fill(128 - slots, -1),
-            seq_lengths,
-            sop_labels,
-            fill(3 * 128 + 124, 0),
-        ]
-    ).reshape(8, 128)
     (wide, tall, head), all_facts, place, found = network.start(
-        (layer_wide.T, layer_tall, head_weights.T), word_table, facts, position_table
+        (layer_wide.T, layer_tall, head_weights.T),
+        word_table,
+        position_table,
+        (token_ids, mlm_labels, mlm_rows, seq_lengths, sop_labels),
     )
     devices = all_facts.shape[0]
     place = place.reshape(-1, E)
@@ -2121,11 +2206,9 @@
             word_table,
             decoder_bias,
             all_facts,
-            facts,
             vec,
         )
     )
-    mlm_count, sop_count = totals[0, 3], totals[0, 4]
     total = vectors.shape[0]
     share = -(-total // (devices * 1024)) * 1024
     back_rows, back_head, turned, outer, vector_grad = run_backward(
@@ -2176,7 +2259,9 @@
         + (LEARN_RATE,),
         (lines(vectors), lines(vector_first), lines(vector_second), last, None, SMALL_RATE),
     )
-    word, wide, tall, head, position, decoder, vector = network.adam(ends, groups)
+    arrays, scalars = network.adam(ends, groups)
+    word, wide, tall, head, position, decoder, vector = arrays
+    grad_norm, unused, mlm_sum, sop_total, mlm_count, sop_count = scalars
 
     def turn(arrays):
         return [x.T for x in arrays]
@@ -2185,7 +2270,6 @@
         return [x.reshape(-1) for x in arrays]
 
     updates = (*word, *position, *turn(head), *plain(decoder), *turn(wide), *tall, *plain(vector))
-    grad_norm, mlm_sum, sop_total = ends[0, 0], ends[2, 0], ends[3, 0]
     return (*updates, mlm_sum, mlm_count, sop_total, sop_count, grad_norm)
 
 

time: 335 us -> 315 us (0.940)
  Pallas kernels: 330 us -> 314 us
    pallas_call x1, Pallas kernels: 97.8 us -> 85.7 us  [run_finish(): pl.pallas_call(functools.partial(finish_kernel, planes, heights, split),...]
where the time goes in v1:
time: 315 us
  Pallas kernels  314 us (100%)
    pallas_call x1, Pallas kernels, run_start(): pl.pallas_call(functools.partial(start_kernel, planes, rows, tuple(member...  85.9 us
    pallas_call x1, Pallas kernels, run_finish(): pl.pallas_call(functools.partial(finish_kernel, planes, heights, split),...  85.7 us
    pallas_call x1, Pallas kernels, run_forward(): pl.pallas_call(forward_kernel, grid=(LAYERS,), out_shape=[jax.ShapeDtypeS...  45.8 us
    pallas_call x1, Pallas kernels, run_backward(): pl.pallas_call(backward_kernel, grid=(LAYERS,), out_shape=[jax.ShapeDtype...  45.5 us
    pallas_call x1, Pallas kernels, run_head(): pl.pallas_call(functools.partial(head_kernel, planes), out_shape=[jax.Sha...  44 us
    pallas_call x1, Pallas kernels, run_adam(): pl.pallas_call(functools.partial(adam_kernel, blocks, tuple((group[5] for...  6.95 us

profile of v1, /device:TPU:0, one launch (start us, length us, event | category | flops | bytes accessed | tf_op | source)
XLA Modules:
  0.0 314.7 jit_solution(13279802157309171511)
XLA Ops:
  0.7 85.9 %shard_map.449 = (bf16[4,4,2,192,768]{4,3,2,1,0:T(8,128)(2,1)}, bf16[4,4,2,96,768]{4,3,2,1,0:T(8,128)(2,1)}, bf16[4,4,2,32,768]{4,3,2,1,0:T(8,128)(2,1)}, s32[4,...) custom-call(f32[192,768]{1,0:T(8,128)} %bitcast.50, f32[96,768]{1,0:T(8,128)} %refs_9_.1, ...), custom_call_target="tpu_custom_call" | custom-call | tf_op jit(solution)/shard_map/pallas_call | solution.py:489
  86.6 45.8 %shard_map.450 = (f32[256,768]{1,0:T(8,128)}, f32[256,128]{1,0:T(8,128)}, f32[256,1]{1,0:T(8,128)}, bf16[256,128]{1,0:T(8,128)(2,1)}, bf16[3,4,256,768]{3,2,1,0:...) custom-call(s32[2]{0:T(128)} %lengths.7, ...), custom_call_target="tpu_custom_call" | custom-call | tf_op jit(solution)/shard_map/pallas_call | solution.py:1910
  132.3 44.0 %shard_map.451 = (f32[256,768]{1,0:T(8,128)}, f32[960,128]{1,0:T(8,128)}, f32[1,960]{1,0:T(1,128)}, bf16[1024,768]{1,0:T(8,128)(2,1)}, f32[3,768]{1,0:T(4,128)}, /*index=5*/f32[3,128]{1,0:T(4,128)}, f32[1,128]{1,0:T(1,128)}) custom-call(s32[2]{0:T(128)} %lengths.7, s32[2]{0:T(128)} %sop_labels.3, f32[256,768]{1,0:T(8,128)} %get-tuple-element.93.final, ...), custom_call_target="tpu_custom_call" | custom-call | tf_op jit(solution)/shard_map/pallas_call | solution.py:1422
  176.4 45.5 %shard_map.452 = (bf16[256,128]{1,0:T(8,128)(2,1)}, bf16[1024,768]{1,0:T(8,128)(2,1)}, bf16[6144,1024]{1,0:T(8,128)(2,1)}, bf16[4,256,768]{2,1,0:T(8,128)(2,1)}, f32[256,128]{1,0:T(8,128)}) custom-call(s32[2]{0:T(128)} %lengths.7, f32[256,768]{1,0:T(8,128)} %get-tuple-element.95.start, ...), custom_call_target="tpu_custom_call", output_to_operand_aliasing={{1}: (8, {})} | custom-call | tf_op jit(solution)/shard_map/pallas_call | solution.py:2095
  221.9 85.7 %shard_map.453 = (f32[320,768]{1,0:T(8,128)}, f32[960,128]{1,0:T(8,128)}, f32[16,128]{1,0:T(8,128)}, f32[4,8,16,128]{3,2,1,0:T(8,128)}, f32[8,128]{1,0:T(8,128)}) custom-call(bf16[6144,1024]{1,0:T(8,128)(2,1)} %get-tuple-element.109.left_wide, bf16[3072,1024]{1,0:T(8,128)(2,1)} %get-tuple-element.110.left_tall, bf16[3,1024,768]{2,1,0:T(8,128)(2,1)} %bitcast.49, ...), custom_call_target="tpu_custom_call" | custom-call | tf_op jit(solution)/shard_map/pallas_call | solution.py:1103
  307.6 7.0 %shard_map.454 = (f32[960,128]{1,0:T(8,128)}, f32[960,128]{1,0:T(8,128)}, f32[960,128]{1,0:T(8,128)}, f32[192,768]{1,0:T(8,128)}, f32[192,768]{1,0:T(8,128)}, /*...) custom-call(f32[8,128]{1,0:T(8,128)} %get-tuple-element.119.refs_0_,, ...), custom_call_target="tpu_custom_call" | custom-call | tf_op jit(solution)/shard_map/pallas_call | solution.py:1516

commit v2 on v1

--- a/solution.py
+++ b/solution.py
@@ -1314,8 +1314,15 @@
     tops, sums, targets = [], [], []
     chunk = width * WIRE
     flat_t = all_t[...].reshape(slots, E)
+
+    def logits_of(low):
+        return nt(word_half[...], flat_t[low : low + chunk])
+
+    coming = logits_of(0)
     for low in range(0, slots, chunk):
-        logits = nt(word_half[...], flat_t[low : low + chunk]) + bias
+        logits = coming + bias
+        if low + chunk < slots:
+            coming = logits_of(low + chunk)
         top = jnp.max(logits, 0, keepdims=True)
         power = jnp.exp(logits - top)
         powers[:, pl.ds(low, chunk)] = power
@@ -1352,6 +1359,13 @@
             who,
         )
 
+    def spread(word_sums, words_total, low, half):
+        zz = low // chunk
+        back_t[zz] = tn(half, word_half[...]).reshape(width, WIRE, E)
+        start([slot_terms(zz, d, who) for d, who in enumerate(plane)])
+        return word_sums + nt(ones, half), words_total + nn(half, flat_t[low : low + chunk])
+
+    ready = []
     words_total = jnp.zeros((words, E), single)
     word_sums = jnp.zeros((8, words), single)
     ones = jnp.ones((8, width * WIRE), jnp.bfloat16)
@@ -1363,12 +1377,10 @@
                 mark, weight[:, at : at + 128], 0.0
             )
             parts.append(to_half(part))
-        half = jnp.concatenate(parts, 1)
-        word_sums = word_sums + nt(ones, half)
-        words_total = words_total + nn(half, flat_t[low : low + chunk])
-        zz = low // chunk
-        back_t[zz] = tn(half, word_half[...]).reshape(width, WIRE, E)
-        start([slot_terms(zz, d, who) for d, who in enumerate(plane)])
+        if ready:
+            word_sums, words_total = spread(word_sums, words_total, *ready.pop())
+        ready.append((low, jnp.concatenate(parts, 1)))
+    word_sums, words_total = spread(word_sums, words_total, *ready.pop())
     back_word[...] = words_total
     back_decoder[...] = word_sums[0:1]
 
@@ -1741,7 +1753,7 @@
     return lax.dot_general(a, b, (((0,), (0,)), ((), ())), preferred_element_type=jnp.float32)
 
 
-CHUNK = 512
+FORWARD_CHUNK, BACKWARD_CHUNK = 1024, 256
 PAIR = 2 * HEAD_DIM
 PROJ_B, Q_B, V_B, O_B, LN1_G, LN1_B, FFO_B, LN2_G, LN2_B, POOL_B = range(10)
 
@@ -1833,19 +1845,33 @@
                 value = value + lanes_of(vec, (bias * D + low) // 128, 2)
             projected[:, pl.ds(here, 256)] = to_half(value)
     allowed = allowed_block(lengths)
-    for pair in range(HEADS // 2):
-        lanes = pair * PAIR
-        queries = halves(projected[:, pl.ds(lanes, PAIR)])
-        keys = projected[:, pl.ds(D + lanes, PAIR)]
-        values = halves_down(projected[:, pl.ds(2 * D + lanes, PAIR)].T)
-        total = jnp.zeros((PAIR, ROWS), jnp.float32)
-        for side in (0, 1):
-            scores = jnp.where(allowed, nt(keys, queries[side]) * SCALE, MASKED)
-            powers = jnp.exp(scores - jnp.max(scores, 0, keepdims=True))
-            weights = powers * (1.0 / jnp.sum(powers, 0, keepdims=True))
-            weighting[2 * pair + side] = weights
-            total = total + nn(values[side], to_half(weights))
-        rights[1, :, pl.ds(lanes, PAIR)] = to_half(total).T
+    def scores_of(head):
+        lanes = head // 2 * PAIR
+        queries = halves(projected[:, pl.ds(lanes, PAIR)])[head % 2]
+        return nt(projected[:, pl.ds(D + lanes, PAIR)], queries)
+
+    def mix(head, weights):
+        lanes = head // 2 * PAIR
+        values = halves_down(projected[:, pl.ds(2 * D + lanes, PAIR)].T)[head % 2]
+        part = nn(values, weights)
+        if head % 2:
+            rights[1, :, pl.ds(lanes, PAIR)] = to_half(mixes.pop() + part).T
+        else:
+            mixes.append(part)
+
+    mixes, waiting, coming = [], None, scores_of(0)
+    for head in range(HEADS):
+        products = coming
+        if head + 1 < HEADS:
+            coming = scores_of(head + 1)
+        scores = jnp.where(allowed, products * SCALE, MASKED)
+        powers = jnp.exp(scores - jnp.max(scores, 0, keepdims=True))
+        weights = powers * (1.0 / jnp.sum(powers, 0, keepdims=True))
+        weighting[head] = weights
+        if waiting is not None:
+            mix(head - 1, waiting)
+        waiting = to_half(weights)
+    mix(HEADS - 1, waiting)
     first_sum = hidden[...] + nt(rights[1], wide[pl.ds(3 * D, D), :]) + row(O_B)
     hat, inverse = norm_forward(first_sum)
     hat_one[...] = hat
@@ -1854,17 +1880,23 @@
     half = to_half(middle)
     rights[2] = half
     total = middle + row(FFO_B)
-    for low in range(0, FF, CHUNK):
-        bias = lanes_of(vec, FF_AT + low // 128, CHUNK // 128)
-        inner = nt(half, wide[pl.ds(4 * D + low, CHUNK), :]) + bias
+
+    def inner_of(low):
+        return nt(half, wide[pl.ds(4 * D + low, FORWARD_CHUNK), :])
+
+    coming = inner_of(0)
+    for low in range(0, FF, FORWARD_CHUNK):
+        inner = coming + lanes_of(vec, FF_AT + low // 128, FORWARD_CHUNK // 128)
+        if low + FORWARD_CHUNK < FF:
+            coming = inner_of(low + FORWARD_CHUNK)
         square = inner * inner
         bend = jnp.tanh(GELU_A * inner * (1.0 + GELU_B * square))
         act = to_half(0.5 * inner * (1.0 + bend))
-        slope[:, pl.ds(low, CHUNK)] = 0.5 * (1.0 + bend) + (0.5 * GELU_A) * inner * (
+        slope[:, pl.ds(low, FORWARD_CHUNK)] = 0.5 * (1.0 + bend) + (0.5 * GELU_A) * inner * (
             1.0 - bend * bend
         ) * (1.0 + 3.0 * GELU_B * square)
-        active[pl.ds(low, CHUNK), :] = act.T
-        total = total + nn(act, tall[pl.ds(low, CHUNK), :])
+        active[pl.ds(low, FORWARD_CHUNK), :] = act.T
+        total = total + nn(act, tall[pl.ds(low, FORWARD_CHUNK), :])
     hat, inverse = norm_forward(total)
     hat_two[...] = hat
     inverse_two[...] = inverse
@@ -2007,14 +2039,22 @@
     outer[...] = half
     add_sum(FFO_B, half.astype(jnp.float32))
     total = back_second
-    for low in range(0, FF, CHUNK):
-        lanes = pl.ds(low, CHUNK)
-        inner = to_half(nt(half, tall[lanes, :]) * slope[:, lanes])
+
+    def back_active(low):
+        return nt(half, tall[pl.ds(low, BACKWARD_CHUNK), :])
+
+    coming = back_active(0)
+    for low in range(0, FF, BACKWARD_CHUNK):
+        lanes = pl.ds(low, BACKWARD_CHUNK)
+        product = coming
+        if low + BACKWARD_CHUNK < FF:
+            coming = back_active(low + BACKWARD_CHUNK)
+        inner = to_half(product * slope[:, lanes])
         ff_sum[:, lanes] = ff_sum[:, lanes] + jnp.sum(
             inner.astype(jnp.float32), 0, keepdims=True
         )
-        turned[pl.ds(4 * D + low, CHUNK), :] = inner.T
-        total = total + nn(inner, wide[pl.ds(4 * D + low, CHUNK), :])
+        turned[pl.ds(4 * D + low, BACKWARD_CHUNK), :] = inner.T
+        total = total + nn(inner, wide[pl.ds(4 * D + low, BACKWARD_CHUNK), :])
     hat = hat_one[...]
     add_sum(LN1_G, total * hat)
     add_sum(LN1_B, total)
@@ -2024,29 +2064,42 @@
     add_sum(O_B, half.astype(jnp.float32))
     turned[pl.ds(3 * D, D), :] = half.T
     back_mixed[...] = to_half(nn(half, wide[pl.ds(3 * D, D), :]))
-    for pair in range(HEADS // 2):
-        lanes = pair * PAIR
-        queries = halves(projected[:, pl.ds(lanes, PAIR)])
-        keys = halves_down(projected[:, pl.ds(D + lanes, PAIR)].T)
-        values = projected[:, pl.ds(2 * D + lanes, PAIR)]
-        grads = halves(back_mixed[:, pl.ds(lanes, PAIR)])
-        zero = jnp.zeros((ROWS, PAIR), jnp.float32)
-        back_query, back_key, back_value = jnp.zeros((PAIR, ROWS), jnp.float32), zero, zero
-        for side in (0, 1):
-            weights = weighting[2 * pair + side]
-            soft = nt(values, grads[side])
-            scores = to_half(weights * (soft - jnp.sum(weights * soft, 0, keepdims=True)))
-            back_query = back_query + nn(keys[side], scores)
-            back_key = back_key + nn(scores, queries[side])
-            back_value = back_value + nn(to_half(weights), grads[side])
-        query_half = to_half(back_query * SCALE)
-        key_half, value_half = to_half(back_key * SCALE), to_half(back_value)
+
+    def soft_of(head):
+        lanes = head // 2 * PAIR
+        grads = halves(back_mixed[:, pl.ds(lanes, PAIR)])[head % 2]
+        return nt(projected[:, pl.ds(2 * D + lanes, PAIR)], grads)
+
+    def spread(head, scores, weights):
+        lanes, side = head // 2 * PAIR, head % 2
+        queries = halves(projected[:, pl.ds(lanes, PAIR)])[side]
+        keys = halves_down(projected[:, pl.ds(D + lanes, PAIR)].T)[side]
+        grads = halves(back_mixed[:, pl.ds(lanes, PAIR)])[side]
+        parts = nn(keys, scores), nn(scores, queries), nn(weights, grads)
+        if side == 0:
+            sides.extend(parts)
+            return
+        value_half = to_half(sides.pop() + parts[2])
+        key_half = to_half((sides.pop() + parts[1]) * SCALE)
+        query_half = to_half((sides.pop() + parts[0]) * SCALE)
         joint[:, pl.ds(lanes, PAIR)] = query_half.T
         joint[:, pl.ds(D + lanes, PAIR)] = key_half
         joint[:, pl.ds(2 * D + lanes, PAIR)] = value_half
         turned[pl.ds(lanes, PAIR), :] = query_half
         turned[pl.ds(D + lanes, PAIR), :] = key_half.T
         turned[pl.ds(2 * D + lanes, PAIR), :] = value_half.T
+
+    sides, waiting, coming = [], None, soft_of(0)
+    for head in range(HEADS):
+        soft = coming
+        if head + 1 < HEADS:
+            coming = soft_of(head + 1)
+        weights = weighting[head]
+        scores = to_half(weights * (soft - jnp.sum(weights * soft, 0, keepdims=True)))
+        if waiting is not None:
+            spread(head - 1, *waiting)
+        waiting = (scores, to_half(weights))
+    spread(HEADS - 1, *waiting)
     total = upstream[...]
     for part, bias in ((0, Q_B), (1, None), (2, V_B)):
         here = pl.ds(part * D, D)

time: 315 us -> 305 us (0.968)
  Pallas kernels: 314 us -> 303 us
    pallas_call x1, Pallas kernels: 45.5 us -> 40 us  [run_backward(): pl.pallas_call(backward_kernel, grid=(LAYERS,), out_shape=[jax.ShapeDtype...]
    pallas_call x1, Pallas kernels: 45.8 us -> 41.4 us  [run_forward(): pl.pallas_call(forward_kernel, grid=(LAYERS,), out_shape=[jax.ShapeDtypeS...]
where the time goes in v2:
time: 305 us; the launch traced here: 304 us
  Pallas kernels  303 us (99%)
    pallas_call x1, Pallas kernels, run_start(): pl.pallas_call(functools.partial(start_kernel, planes, rows, tuple(member...  85.9 us
    pallas_call x1, Pallas kernels, run_finish(): pl.pallas_call(functools.partial(finish_kernel, planes, heights, split),...  85.7 us
    pallas_call x1, Pallas kernels, run_head(): pl.pallas_call(functools.partial(head_kernel, planes), out_shape=[jax.Sha...  43.6 us
    pallas_call x1, Pallas kernels, run_forward(): pl.pallas_call(forward_kernel, grid=(LAYERS,), out_shape=[jax.ShapeDtypeS...  41.4 us
    pallas_call x1, Pallas kernels, run_backward(): pl.pallas_call(backward_kernel, grid=(LAYERS,), out_shape=[jax.ShapeDtype...  40 us
    pallas_call x1, Pallas kernels, run_adam(): pl.pallas_call(functools.partial(adam_kernel, blocks, tuple((group[5] for...  6.95 us

profile of v2, /device:TPU:0, one launch (start us, length us, event | category | flops | bytes accessed | tf_op | source)
XLA Modules:
  0.0 304.4 jit_solution(11158817458512039800)
XLA Ops:
  0.7 85.9 %shard_map.449 = (bf16[4,4,2,192,768]{4,3,2,1,0:T(8,128)(2,1)}, bf16[4,4,2,96,768]{4,3,2,1,0:T(8,128)(2,1)}, bf16[4,4,2,32,768]{4,3,2,1,0:T(8,128)(2,1)}, s32[4,...) custom-call(f32[192,768]{1,0:T(8,128)} %bitcast.50, f32[96,768]{1,0:T(8,128)} %refs_9_.1, ...), custom_call_target="tpu_custom_call" | custom-call | tf_op jit(solution)/shard_map/pallas_call | solution.py:489
  86.6 41.4 %shard_map.450 = (f32[256,768]{1,0:T(8,128)}, f32[256,128]{1,0:T(8,128)}, f32[256,1]{1,0:T(8,128)}, bf16[256,128]{1,0:T(8,128)(2,1)}, bf16[3,4,256,768]{3,2,1,0:...) custom-call(s32[2]{0:T(128)} %lengths.7, ...), custom_call_target="tpu_custom_call" | custom-call | tf_op jit(solution)/shard_map/pallas_call | solution.py:1942
  127.9 43.6 %shard_map.451 = (f32[256,768]{1,0:T(8,128)}, f32[960,128]{1,0:T(8,128)}, f32[1,960]{1,0:T(1,128)}, bf16[1024,768]{1,0:T(8,128)(2,1)}, f32[3,768]{1,0:T(4,128)}, /*index=5*/f32[3,128]{1,0:T(4,128)}, f32[1,128]{1,0:T(1,128)}) custom-call(s32[2]{0:T(128)} %lengths.7, s32[2]{0:T(128)} %sop_labels.3, f32[256,768]{1,0:T(8,128)} %get-tuple-element.93.final, ...), custom_call_target="tpu_custom_call" | custom-call | tf_op jit(solution)/shard_map/pallas_call | solution.py:1434
  171.5 40.0 %shard_map.452 = (bf16[256,128]{1,0:T(8,128)(2,1)}, bf16[1024,768]{1,0:T(8,128)(2,1)}, bf16[6144,1024]{1,0:T(8,128)(2,1)}, bf16[4,256,768]{2,1,0:T(8,128)(2,1)}, f32[256,128]{1,0:T(8,128)}) custom-call(s32[2]{0:T(128)} %lengths.7, f32[256,768]{1,0:T(8,128)} %get-tuple-element.95.start, ...), custom_call_target="tpu_custom_call", output_to_operand_aliasing={{1}: (8, {})} | custom-call | tf_op jit(solution)/shard_map/pallas_call | solution.py:2148
  211.5 85.7 %shard_map.453 = (f32[320,768]{1,0:T(8,128)}, f32[960,128]{1,0:T(8,128)}, f32[16,128]{1,0:T(8,128)}, f32[4,8,16,128]{3,2,1,0:T(8,128)}, f32[8,128]{1,0:T(8,128)}) custom-call(bf16[6144,1024]{1,0:T(8,128)(2,1)} %get-tuple-element.109.left_wide, bf16[3072,1024]{1,0:T(8,128)(2,1)} %get-tuple-element.110.left_tall, bf16[3,1024,768]{2,1,0:T(8,128)(2,1)} %bitcast.49, ...), custom_call_target="tpu_custom_call" | custom-call | tf_op jit(solution)/shard_map/pallas_call | solution.py:1103
  297.2 7.0 %shard_map.454 = (f32[960,128]{1,0:T(8,128)}, f32[960,128]{1,0:T(8,128)}, f32[960,128]{1,0:T(8,128)}, f32[192,768]{1,0:T(8,128)}, f32[192,768]{1,0:T(8,128)}, /*...) custom-call(f32[8,128]{1,0:T(8,128)} %get-tuple-element.119.refs_0_,, ...), custom_call_target="tpu_custom_call" | custom-call | tf_op jit(solution)/shard_map/pallas_call | solution.py:1528

commit v3 on v2

--- a/solution.py
+++ b/solution.py
@@ -369,7 +369,7 @@
         line_message(d, who).wait_send()
 
 
-PLAN = (1, 1, 1, 1, 1, 1, 1, 1, 1, 1, 1, 1, 1, 1)
+PLAN = (1, 2, 1, 1, 0, 1, 0, 0, 0, 0, 1)
 
 
 def start_kernel(
@@ -1502,6 +1502,9 @@
             scalar[0] = jnp.sum(jnp.where(lane == 0, ends[at : at + 1, :], 0.0))
 
 
+ADAM_STEPS = 2
+
+
 def run_adam(ends, groups, steps):
     in_specs = [pl.BlockSpec(ends.shape, lambda i: (0, 0))]
     out_specs, shapes, given = [], [], [ends]
@@ -1644,7 +1647,7 @@
 
     def adam(self, ends, groups):
         if self.kernels:
-            updates = run_adam(ends, groups, 4)
+            updates = run_adam(ends, groups, ADAM_STEPS)
             scalars = [x.reshape(()) for x in updates[-6:]]
             return [updates[i : i + 3] for i in range(0, 3 * len(groups), 3)], scalars
         updates = []
@@ -1753,7 +1756,7 @@
     return lax.dot_general(a, b, (((0,), (0,)), ((), ())), preferred_element_type=jnp.float32)
 
 
-FORWARD_CHUNK, BACKWARD_CHUNK = 1024, 256
+FORWARD_CHUNK, BACKWARD_CHUNK = 768, 256
 PAIR = 2 * HEAD_DIM
 PROJ_B, Q_B, V_B, O_B, LN1_G, LN1_B, FFO_B, LN2_G, LN2_B, POOL_B = range(10)
 

time: 305 us -> 303 us (level)
  no operation moved by 1% of the time
where the time goes in v3:
time: 303 us
  Pallas kernels  302 us (100%)
    pallas_call x1, Pallas kernels, run_finish(): pl.pallas_call(functools.partial(finish_kernel, planes, heights, split),...  86.4 us
    pallas_call x1, Pallas kernels, run_start(): pl.pallas_call(functools.partial(start_kernel, planes, rows, tuple(member...  84 us
    pallas_call x1, Pallas kernels, run_head(): pl.pallas_call(functools.partial(head_kernel, planes), out_shape=[jax.Sha...  44.8 us
    pallas_call x1, Pallas kernels, run_forward(): pl.pallas_call(forward_kernel, grid=(LAYERS,), out_shape=[jax.ShapeDtypeS...  40.4 us
    pallas_call x1, Pallas kernels, run_backward(): pl.pallas_call(backward_kernel, grid=(LAYERS,), out_shape=[jax.ShapeDtype...  40 us
    pallas_call x1, Pallas kernels, run_adam(): pl.pallas_call(functools.partial(adam_kernel, blocks, tuple((group[5] for...  6.27 us

profile of v3, /device:TPU:0, one launch (start us, length us, event | category | flops | bytes accessed | tf_op | source)
XLA Modules:
  0.0 302.8 jit_solution(2142139656277751263)
XLA Ops:
  0.7 84.0 %shard_map.449 = (bf16[4,4,2,192,768]{4,3,2,1,0:T(8,128)(2,1)}, bf16[4,4,2,96,768]{4,3,2,1,0:T(8,128)(2,1)}, bf16[4,4,2,32,768]{4,3,2,1,0:T(8,128)(2,1)}, s32[4,...) custom-call(f32[192,768]{1,0:T(8,128)} %bitcast.50, f32[96,768]{1,0:T(8,128)} %refs_9_.1, ...), custom_call_target="tpu_custom_call" | custom-call | tf_op jit(solution)/shard_map/pallas_call | solution.py:489
  84.7 40.4 %shard_map.450 = (f32[256,768]{1,0:T(8,128)}, f32[256,128]{1,0:T(8,128)}, f32[256,1]{1,0:T(8,128)}, bf16[256,128]{1,0:T(8,128)(2,1)}, bf16[3,4,256,768]{3,2,1,0:...) custom-call(s32[2]{0:T(128)} %lengths.7, ...), custom_call_target="tpu_custom_call" | custom-call | tf_op jit(solution)/shard_map/pallas_call | solution.py:1945
  125.1 44.8 %shard_map.451 = (f32[256,768]{1,0:T(8,128)}, f32[960,128]{1,0:T(8,128)}, f32[1,960]{1,0:T(1,128)}, bf16[1024,768]{1,0:T(8,128)(2,1)}, f32[3,768]{1,0:T(4,128)}, /*index=5*/f32[3,128]{1,0:T(4,128)}, f32[1,128]{1,0:T(1,128)}) custom-call(s32[2]{0:T(128)} %lengths.7, s32[2]{0:T(128)} %sop_labels.3, f32[256,768]{1,0:T(8,128)} %get-tuple-element.93.final, ...), custom_call_target="tpu_custom_call" | custom-call | tf_op jit(solution)/shard_map/pallas_call | solution.py:1434
  169.9 40.0 %shard_map.452 = (bf16[256,128]{1,0:T(8,128)(2,1)}, bf16[1024,768]{1,0:T(8,128)(2,1)}, bf16[6144,1024]{1,0:T(8,128)(2,1)}, bf16[4,256,768]{2,1,0:T(8,128)(2,1)}, f32[256,128]{1,0:T(8,128)}) custom-call(s32[2]{0:T(128)} %lengths.7, f32[256,768]{1,0:T(8,128)} %get-tuple-element.95.start, ...), custom_call_target="tpu_custom_call", output_to_operand_aliasing={{1}: (8, {})} | custom-call | tf_op jit(solution)/shard_map/pallas_call | solution.py:2151
  209.9 86.4 %shard_map.453 = (f32[320,768]{1,0:T(8,128)}, f32[960,128]{1,0:T(8,128)}, f32[16,128]{1,0:T(8,128)}, f32[4,8,16,128]{3,2,1,0:T(8,128)}, f32[8,128]{1,0:T(8,128)}) custom-call(bf16[6144,1024]{1,0:T(8,128)(2,1)} %get-tuple-element.109.left_wide, bf16[3072,1024]{1,0:T(8,128)(2,1)} %get-tuple-element.110.left_tall, bf16[3,1024,768]{2,1,0:T(8,128)(2,1)} %bitcast.49, ...), custom_call_target="tpu_custom_call" | custom-call | tf_op jit(solution)/shard_map/pallas_call | solution.py:1103
  296.3 6.3 %shard_map.454 = (f32[960,128]{1,0:T(8,128)}, f32[960,128]{1,0:T(8,128)}, f32[960,128]{1,0:T(8,128)}, f32[192,768]{1,0:T(8,128)}, f32[192,768]{1,0:T(8,128)}, /*...) custom-call(f32[8,128]{1,0:T(8,128)} %get-tuple-element.119.refs_0_,, ...), custom_call_target="tpu_custom_call" | custom-call | tf_op jit(solution)/shard_map/pallas_call | solution.py:1531
